TPU v7x, 32 devices: a whole 2x2x4 slice. The times are simulated.
32 devices in a mesh: dp: 8 (over z, y), fsdp: 4 (over x, core).
Axes of the slice: x: 2, y: 2, z: 4, core: 2. Of those that a mesh axis runs over, the one named last changes fastest.
Arguments:
- tokens: bfloat16 [64, 192, 1024], P(('dp', 'fsdp')), may hold values from -6 to 6
- encoder: bfloat16 [64, 384, 1024], P(('dp', 'fsdp')), may hold values from -6 to 6
- cotangent: bfloat16 [64, 192, 1024], P(('dp', 'fsdp')), may hold values from -6 to 6
- lengths: int32 [64], P(('dp', 'fsdp')), may hold values from 48 to 192
- enc_lengths: int32 [64], P(('dp', 'fsdp')), may hold values from 96 to 384
- bucket_ids: int32 [192], replicated, may hold values from 0 to 31
- self_qkv: bfloat16 [1024, 3072], P(('dp', 'fsdp')), may hold values from -0.1875 to 0.1875
- self_out: bfloat16 [1024, 1024], P(('dp', 'fsdp')), may hold values from -0.5 to 0.5
- cross_q: bfloat16 [1024, 1024], P(('dp', 'fsdp')), may hold values from -0.1875 to 0.1875
- cross_kv: bfloat16 [1024, 2048], P(('dp', 'fsdp')), may hold values from -0.1875 to 0.1875
- cross_out: bfloat16 [1024, 1024], P(('dp', 'fsdp')), may hold values from -0.5 to 0.5
- ff_in: bfloat16 [1024, 5632], P(('dp', 'fsdp')), may hold values from -0.1875 to 0.1875
- ff_out: bfloat16 [2816, 1024], P(('dp', 'fsdp')), may hold values from -0.109375 to 0.109375
- norm_gains: bfloat16 [3, 1024], P(None, ('dp', 'fsdp')), may hold values from 0.5 to 1.5
- rel_bias: bfloat16 [512], P(('dp', 'fsdp')), may hold values from -4 to 4
Outputs:
- output: float32 [64, 192, 1024], P(('dp', 'fsdp'))
- grad_tokens: float32 [64, 192, 1024], P(('dp', 'fsdp'))
- grad_encoder: float32 [64, 384, 1024], P(('dp', 'fsdp'))
- grad_self_qkv: float32 [1024, 3072], P(('dp', 'fsdp'))
- grad_self_out: float32 [1024, 1024], P(('dp', 'fsdp'))
- grad_cross_q: float32 [1024, 1024], P(('dp', 'fsdp'))
- grad_cross_kv: float32 [1024, 2048], P(('dp', 'fsdp'))
- grad_cross_out: float32 [1024, 1024], P(('dp', 'fsdp'))
- grad_ff_in: float32 [1024, 5632], P(('dp', 'fsdp'))
- grad_ff_out: float32 [2816, 1024], P(('dp', 'fsdp'))
- grad_norm_gains: float32 [3, 1024], P(None, ('dp', 'fsdp'))
- grad_rel_bias: float32 [512], P(('dp', 'fsdp'))
All inputs are finite; a program needn't handle non-finite values.
Results may differ from a plain program's by a relative error of at most 0.022.
Values may be sent and summed in bfloat16 or wider, within the bound.
A program may use at most 200 MiB of HBM per device.

v0:
```python
import jax
import jax.numpy as jnp
from jax import lax
from jax.sharding import PartitionSpec as P

HEADS = 16
HEAD = 64
BUCKETS = 32


def norm_scale(stream, gain):
    return stream * lax.rsqrt(jnp.mean(stream * stream, axis=-1, keepdims=True) + 1e-06) * gain


def gelu_tanh(values):
    return (
        0.5
        * values
        * (1.0 + jnp.tanh(0.7978845608028654 * (values + 0.044715 * values * values * values)))
    )


def gated(gate_up):
    half_width = gate_up.shape[1] // 2
    return gelu_tanh(gate_up[:, :half_width]) * gate_up[:, half_width:]


def masked_scores(queries, key_rows, pos_bias, keep_mask):
    scores = jnp.einsum(
        "ihc,jhc->hij", queries, key_rows, preferred_element_type=jnp.float32
    ) * HEAD ** (-0.5)
    if pos_bias is not None:
        scores = scores + pos_bias
    return jnp.where(keep_mask[None], scores, -1e30)


def attend_forward(queries, key_rows, value_rows, pos_bias, keep_mask):
    masked = masked_scores(queries, key_rows, pos_bias, keep_mask)
    row_max = jnp.max(masked, axis=-1, keepdims=True)
    totals = jnp.sum(jnp.exp(masked - row_max), axis=-1, keepdims=True)
    log_total = row_max + jnp.log(totals)
    low_probs = jnp.exp(masked - log_total).astype(jnp.bfloat16)
    mixed = jnp.einsum("hij,jhc->ihc", low_probs, value_rows, preferred_element_type=jnp.float32)
    return (mixed.reshape(queries.shape[0], -1).astype(jnp.bfloat16), log_total)


def attend_backward(queries, key_rows, value_rows, pos_bias, keep_mask, log_total, grad_mixed):
    probs = jnp.exp(masked_scores(queries, key_rows, pos_bias, keep_mask) - log_total)
    low_probs = probs.astype(jnp.bfloat16)
    grad_values = jnp.einsum(
        "hij,ihc->jhc", low_probs, grad_mixed, preferred_element_type=jnp.float32
    )
    grad_probs = jnp.einsum(
        "ihc,jhc->hij", grad_mixed, value_rows, preferred_element_type=jnp.float32
    )
    grad_scores = (
        probs * (grad_probs - jnp.sum(probs * grad_probs, axis=-1, keepdims=True))
    ).astype(jnp.bfloat16)
    grad_queries = jnp.einsum(
        "hij,jhc->ihc", grad_scores, key_rows, preferred_element_type=jnp.float32
    ) * HEAD ** (-0.5)
    grad_keys = jnp.einsum(
        "hij,ihc->jhc", grad_scores, queries, preferred_element_type=jnp.float32
    ) * HEAD ** (-0.5)
    return (grad_queries, grad_keys, grad_values, grad_scores)


def fetch_forward(shards):
    self_qkv, self_out, cross_q, cross_kv, cross_out, ff_in, ff_out, norm_gains, rel_bias = shards
    return (
        lax.all_gather(self_qkv, ("dp", "fsdp"), axis=0, tiled=True),
        lax.all_gather(self_out, ("dp", "fsdp"), axis=0, tiled=True),
        lax.all_gather(cross_q, ("dp", "fsdp"), axis=0, tiled=True),
        lax.all_gather(cross_kv, ("dp", "fsdp"), axis=0, tiled=True),
        lax.all_gather(cross_out, ("dp", "fsdp"), axis=0, tiled=True),
        lax.all_gather(ff_in, ("dp", "fsdp"), axis=0, tiled=True),
        lax.all_gather(ff_out, ("dp", "fsdp"), axis=0, tiled=True),
        lax.all_gather(norm_gains, ("dp", "fsdp"), axis=1, tiled=True),
        lax.all_gather(rel_bias, ("dp", "fsdp"), axis=0, tiled=True),
    )


def settle(totals, shards, factor):
    block_sizes = [piece.size for piece in shards]
    per_block = sum(block_sizes)
    blocks = per_block * lax.axis_size(("dp", "fsdp")) // per_block
    pieces = []
    for owner_place, total in enumerate(totals):
        if owner_place == 7:
            width = total.shape[1] // factor
            piece = total
            piece = (
                piece.reshape(total.shape[0], blocks, width).transpose(1, 0, 2).reshape(blocks, -1)
            )
        else:
            piece = total.reshape(blocks, -1)
        pieces.append(piece)
    summed = lax.psum_scatter(
        jnp.concatenate(pieces, axis=1).reshape(-1), ("dp", "fsdp"), scatter_dimension=0, tiled=True
    )
    owned = []
    offset = 0
    for place, shard in enumerate(shards):
        owned.append(summed[offset : offset + block_sizes[place]].reshape(shard.shape))
        offset = offset + block_sizes[place]
    return owned


def widened(array, along, factor):
    dims_list = list(array.shape)
    dims_list[along] = dims_list[along] * factor
    return jnp.zeros(tuple(dims_list), jnp.float32)


def forward_pass(weight_set, tok_rows, enc_rows, length, enc_length, onehot):
    self_qkv, self_out, cross_q, cross_kv, cross_out, ff_in, ff_out, norm_gains, rel_bias = (
        weight_set
    )
    slot_rows = tok_rows.shape[0]
    enc_count = enc_rows.shape[0]
    gain_rows = norm_gains.astype(jnp.float32)
    pos_bias = jnp.dot(
        rel_bias.reshape(HEADS, BUCKETS), onehot, preferred_element_type=jnp.float32
    ).reshape(HEADS, slot_rows, slot_rows)
    row_ids = lax.iota(jnp.int32, slot_rows)
    self_mask = (row_ids[None, :] <= row_ids[:, None]) & (row_ids[None, :] < length)
    cross_mask = jnp.broadcast_to(
        lax.iota(jnp.int32, enc_count)[None, :] < enc_length, (slot_rows, enc_count)
    )
    stream = tok_rows.astype(jnp.float32)
    normed_self, back_self = jax.vjp(norm_scale, stream, gain_rows[0])
    normed_self = normed_self.astype(jnp.bfloat16)
    qkv_all = (
        jnp.dot(normed_self, self_qkv, preferred_element_type=jnp.float32)
        .astype(jnp.bfloat16)
        .reshape(slot_rows, 3, HEADS, HEAD)
    )
    mixed_self, log_self = attend_forward(
        qkv_all[:, 0], qkv_all[:, 1], qkv_all[:, 2], pos_bias, self_mask
    )
    second = stream + jnp.dot(mixed_self, self_out, preferred_element_type=jnp.float32)
    normed_cross, back_cross = jax.vjp(norm_scale, second, gain_rows[1])
    normed_cross = normed_cross.astype(jnp.bfloat16)
    queries = (
        jnp.dot(normed_cross, cross_q, preferred_element_type=jnp.float32)
        .astype(jnp.bfloat16)
        .reshape(slot_rows, HEADS, HEAD)
    )
    enc_pairs = (
        jnp.dot(enc_rows, cross_kv, preferred_element_type=jnp.float32)
        .astype(jnp.bfloat16)
        .reshape(enc_count, 2, HEADS, HEAD)
    )
    mixed_cross, log_cross = attend_forward(
        queries, enc_pairs[:, 0], enc_pairs[:, 1], None, cross_mask
    )
    third = second + jnp.dot(mixed_cross, cross_out, preferred_element_type=jnp.float32)
    normed_ffn, back_ffn = jax.vjp(norm_scale, third, gain_rows[2])
    normed_ffn = normed_ffn.astype(jnp.bfloat16)
    gate_up = jnp.dot(normed_ffn, ff_in, preferred_element_type=jnp.float32)
    activated, back_gate = jax.vjp(gated, gate_up)
    hidden = activated.astype(jnp.bfloat16)
    outcome = third + jnp.dot(hidden, ff_out, preferred_element_type=jnp.float32)
    stored = dict(
        pos_bias=pos_bias,
        self_mask=self_mask,
        cross_mask=cross_mask,
        enc_rows=enc_rows,
        normed_self=normed_self,
        back_self=back_self,
        qkv_all=qkv_all,
        mixed_self=mixed_self,
        log_self=log_self,
        normed_cross=normed_cross,
        back_cross=back_cross,
        queries=queries,
        enc_pairs=enc_pairs,
        mixed_cross=mixed_cross,
        log_cross=log_cross,
        normed_ffn=normed_ffn,
        back_ffn=back_ffn,
        back_gate=back_gate,
        hidden=hidden,
    )
    return (outcome, stored)


def backward_pass(weight_set, stored, cot_rows, length, onehot):
    self_qkv, self_out, cross_q, cross_kv, cross_out, ff_in, ff_out, norm_gains, rel_bias = (
        weight_set
    )
    slot_rows = cot_rows.shape[0]
    enc_count = stored["enc_rows"].shape[0]
    row_ids = lax.iota(jnp.int32, slot_rows)
    grad_out = cot_rows.astype(jnp.float32) * (row_ids < length).astype(jnp.float32)[:, None]
    branch_ffn = grad_out.astype(jnp.bfloat16)
    grad_ff_out = jnp.einsum(
        "lf,ld->fd", stored["hidden"], branch_ffn, preferred_element_type=jnp.float32
    )
    grad_hidden = jnp.einsum("ld,fd->lf", branch_ffn, ff_out, preferred_element_type=jnp.float32)
    (grad_gate_up,) = stored["back_gate"](grad_hidden)
    grad_gate_up = grad_gate_up.astype(jnp.bfloat16)
    grad_ff_in = jnp.einsum(
        "ld,lf->df", stored["normed_ffn"], grad_gate_up, preferred_element_type=jnp.float32
    )
    grad_normed = jnp.einsum("lf,df->ld", grad_gate_up, ff_in, preferred_element_type=jnp.float32)
    grad_stream, gain_ffn = stored["back_ffn"](grad_normed)
    grad_third = grad_out + grad_stream
    branch_cross = grad_third.astype(jnp.bfloat16)
    grad_cross_out = jnp.einsum(
        "le,ld->ed", stored["mixed_cross"], branch_cross, preferred_element_type=jnp.float32
    )
    grad_mixed = (
        jnp.einsum("ld,ed->le", branch_cross, cross_out, preferred_element_type=jnp.float32)
        .astype(jnp.bfloat16)
        .reshape(slot_rows, HEADS, HEAD)
    )
    enc_pairs = stored["enc_pairs"]
    grad_queries, grad_keys, grad_values, unused_scores = attend_backward(
        stored["queries"],
        enc_pairs[:, 0],
        enc_pairs[:, 1],
        None,
        stored["cross_mask"],
        stored["log_cross"],
        grad_mixed,
    )
    grad_query_rows = grad_queries.reshape(slot_rows, -1).astype(jnp.bfloat16)
    grad_pair_rows = (
        jnp.stack([grad_keys, grad_values], axis=1).reshape(enc_count, -1).astype(jnp.bfloat16)
    )
    grad_cross_q = jnp.einsum(
        "ld,le->de", stored["normed_cross"], grad_query_rows, preferred_element_type=jnp.float32
    )
    grad_cross_kv = jnp.einsum(
        "ed,ef->df", stored["enc_rows"], grad_pair_rows, preferred_element_type=jnp.float32
    )
    grad_enc = jnp.einsum("ef,df->ed", grad_pair_rows, cross_kv, preferred_element_type=jnp.float32)
    grad_normed = jnp.einsum(
        "le,de->ld", grad_query_rows, cross_q, preferred_element_type=jnp.float32
    )
    grad_stream, gain_cross = stored["back_cross"](grad_normed)
    grad_second = grad_third + grad_stream
    branch_self = grad_second.astype(jnp.bfloat16)
    grad_self_out = jnp.einsum(
        "le,ld->ed", stored["mixed_self"], branch_self, preferred_element_type=jnp.float32
    )
    grad_mixed = (
        jnp.einsum("ld,ed->le", branch_self, self_out, preferred_element_type=jnp.float32)
        .astype(jnp.bfloat16)
        .reshape(slot_rows, HEADS, HEAD)
    )
    qkv_all = stored["qkv_all"]
    grad_queries, grad_keys, grad_values, grad_scores = attend_backward(
        qkv_all[:, 0],
        qkv_all[:, 1],
        qkv_all[:, 2],
        stored["pos_bias"],
        stored["self_mask"],
        stored["log_self"],
        grad_mixed,
    )
    grad_rel_bias = jnp.einsum(
        "hn,bn->hb",
        grad_scores.reshape(HEADS, slot_rows * slot_rows),
        onehot,
        preferred_element_type=jnp.float32,
    ).reshape(-1)
    grad_qkv = (
        jnp.stack([grad_queries, grad_keys, grad_values], axis=1)
        .reshape(slot_rows, -1)
        .astype(jnp.bfloat16)
    )
    grad_self_qkv = jnp.einsum(
        "ld,lf->df", stored["normed_self"], grad_qkv, preferred_element_type=jnp.float32
    )
    grad_normed = jnp.einsum("lf,df->ld", grad_qkv, self_qkv, preferred_element_type=jnp.float32)
    grad_stream, gain_self = stored["back_self"](grad_normed)
    grad_tok = grad_second + grad_stream
    grad_gains = jnp.stack([gain_self, gain_cross, gain_ffn], axis=0)
    grad_terms = (
        grad_self_qkv,
        grad_self_out,
        grad_cross_q,
        grad_cross_kv,
        grad_cross_out,
        grad_ff_in,
        grad_ff_out,
        grad_gains,
        grad_rel_bias,
    )
    return (grad_terms, grad_tok, grad_enc)


def on_device(
    tokens,
    encoder,
    cotangent,
    lengths,
    enc_lengths,
    bucket_ids,
    self_qkv,
    self_out,
    cross_q,
    cross_kv,
    cross_out,
    ff_in,
    ff_out,
    norm_gains,
    rel_bias,
):
    shards = (self_qkv, self_out, cross_q, cross_kv, cross_out, ff_in, ff_out, norm_gains, rel_bias)
    slot_rows = tokens.shape[1]
    row_ids = lax.iota(jnp.int32, slot_rows)
    distance = jnp.maximum(row_ids[:, None] - row_ids[None, :], 0)
    bucket_map = jnp.take(bucket_ids, distance).reshape(-1)
    onehot = (lax.iota(jnp.int32, BUCKETS)[:, None] == bucket_map[None, :]).astype(jnp.bfloat16)
    factor = lax.axis_size("dp") * lax.axis_size("fsdp")
    initial = (
        widened(self_qkv, 0, factor),
        widened(self_out, 0, factor),
        widened(cross_q, 0, factor),
        widened(cross_kv, 0, factor),
        widened(cross_out, 0, factor),
        widened(ff_in, 0, factor),
        widened(ff_out, 0, factor),
        widened(norm_gains, 1, factor),
        widened(rel_bias, 0, factor),
    )
    held_weights = fetch_forward(shards)

    def micro_step(totals, element):
        tok_rows, enc_rows, cot_rows, length, enc_length = element
        outcome, stored = forward_pass(held_weights, tok_rows, enc_rows, length, enc_length, onehot)
        grad_terms, grad_tok, grad_enc = backward_pass(
            held_weights, stored, cot_rows, length, onehot
        )
        totals = tuple((accum + extra for accum, extra in zip(totals, grad_terms)))
        return (totals, (outcome, grad_tok, grad_enc))

    totals, (outcomes, grad_toks, grad_encs) = lax.scan(
        micro_step, initial, (tokens, encoder, cotangent, lengths, enc_lengths)
    )
    owned = settle(totals, shards, factor)
    return (
        outcomes,
        grad_toks,
        grad_encs,
        owned[0],
        owned[1],
        owned[2],
        owned[3],
        owned[4],
        owned[5],
        owned[6],
        owned[7],
        owned[8],
    )


def solution(mesh):
    placed = (
        P(("dp", "fsdp"), None, None),
        P(("dp", "fsdp"), None, None),
        P(("dp", "fsdp"), None, None),
        P(("dp", "fsdp")),
        P(("dp", "fsdp")),
        P(),
        P(("dp", "fsdp"), None),
        P(("dp", "fsdp"), None),
        P(("dp", "fsdp"), None),
        P(("dp", "fsdp"), None),
        P(("dp", "fsdp"), None),
        P(("dp", "fsdp"), None),
        P(("dp", "fsdp"), None),
        P(None, ("dp", "fsdp")),
        P(("dp", "fsdp")),
    )
    return jax.shard_map(
        on_device,
        mesh=mesh,
        in_specs=placed,
        out_specs=(
            P(("dp", "fsdp"), None, None),
            P(("dp", "fsdp"), None, None),
            P(("dp", "fsdp"), None, None),
            P(("dp", "fsdp"), None),
            P(("dp", "fsdp"), None),
            P(("dp", "fsdp"), None),
            P(("dp", "fsdp"), None),
            P(("dp", "fsdp"), None),
            P(("dp", "fsdp"), None),
            P(("dp", "fsdp"), None),
            P(None, ("dp", "fsdp")),
            P(("dp", "fsdp")),
        ),
        check_vma=False,
    )
```

profile of v0, /device:TPU:0, one launch (start us, length us, event | category | flops | bytes accessed | tf_op | source)
XLA Modules:
  0.0 2018.0 jit_solution(11382383008542039436)
XLA Ops:
  12.6 228.5 %gather_fusion = s32[36864]{0:T(1024)S(1)} fusion(s32[192]{0:T(256)S(1)} %copy-done, s32[36864]{0:T(1024)S(1)} %broadcast_clamp_fusion), kind=kCustom, calls=%fused_computation | custom fusion | bytes 442368 | tf_op jit(solution)/shard_map/jit(_take)/gather | solution.py:316
  247.2 42.9 %all-reduce.2 = bf16[512]{0:T(512)(128)(2,1)S(1)} all-reduce(bf16[512]{0:T(512)(128)(2,1)S(1)} %dynamic-update-slice), channel_id=1, replica_groups=mesh['dp'=8,'fsdp'=4] {'dp','fsdp'}, use_global_device_ids=true, to_apply=%add.2 | all-reduce | flops 512 | bytes 2048
  298.3 40.1 %all-gather = bf16[32,32,3]{1,2,0:T(4,128)(2,1)S(1)} all-gather(bf16[1,32,3]{1,2,0:T(4,128)(2,1)S(1)} %bitcast.405), channel_id=1, replica_groups=mesh['dp'=8,'fsdp'=4] {'dp','fsdp'}, dimensions={0}, use_global_device_ids=true | all-gather | bytes 6336 | tf_op jit(solution)/shard_map/all_gather | solution.py:78
  339.2 50.7 %all-gather.9.cloned.1.call-done = bf16[1024,3072]{1,0:T(8,128)(2,1)} async-done(((bf16[32,3072]{1,0:T(8,128)(2,1)}), bf16[1024,3072]{1,0:T(8,128)(2,1)}) %all-gather.9.cloned.1.call-update) | async-done | bytes 6291472 | tf_op jit(solution)/shard_map/all_gather | solution.py:71
  389.9 92.6 %all-gather.19.cloned.1.call-done = bf16[1024,5632]{1,0:T(8,128)(2,1)} async-done(((bf16[32,5632]{1,0:T(8,128)(2,1)}), bf16[1024,5632]{1,0:T(8,128)(2,1)}) %all-gather.19.cloned.1.call-update) | async-done | bytes 11534352 | tf_op jit(solution)/shard_map/all_gather | solution.py:76
  482.5 329.2 %while.35 = (s32[]{:T(128)}, f32[1024,3072]{1,0:T(8,128)}, f32[1024,1024]{1,0:T(8,128)}, f32[1024,1024]{1,0:T(8,128)}, f32[1024,2048]{1,0:T(8,128)}, /*index=5*/...) while((s32[]{:T(128)}, f32[1024,3072]{1,0:T(8,128)}, ...), condition=%wide.region_16.17_spmd.clone, body=%wide.region_0.16_spmd.clone.sunk | while | flops 23560857600 | bytes 855100928 | solution.py:341
  523.1 15.9 fusion.258
  539.0 10.2 multiply_reduce_fusion.16
  578.2 11.9 select_add_fusion.21
  595.6 6.7 select_add_fusion.19
  688.5 10.2 multiply_reduce_fusion.16
  727.7 16.2 select_add_fusion.21
  749.3 10.2 select_add_fusion.19
  795.6 10.4 select_add_fusion.22
  811.7 9.9 reshape.395
  821.5 10.2 constant_dynamic-update-slice_fusion.6
  841.7 7.5 reshape.398
  854.2 24.7 %reshape.400 = f32[32,180224]{1,0:T(8,128)} reshape(f32[1024,5632]{1,0:T(8,128)} %get-tuple-element.995) | data formatting | bytes 46137344 | tf_op jit(solution)/shard_map/reshape | solution.py:96
  878.9 9.5 reshape.401
  897.9 7.8 constant_dynamic-update-slice_fusion.3
  910.4 8.2 constant_dynamic-update-slice_fusion.1
  918.6 9.2 constant_dynamic-update-slice_fusion
  930.8 82.4 %reshape.405 = f32[17042944]{0:T(1024)} reshape(f32[32,532592]{1,0:T(8,128)} %dynamic-update-slice.9) | data formatting | bytes 136343552 | tf_op jit(solution)/shard_map/reshape | solution.py:99
  1013.3 983.6 %all-reduce.6.cloned.1.call-done = f32[17042944]{0:T(1024)} async-done(((f32[17042944]{0:T(1024)}), f32[17042944]{0:T(1024)}) %all-reduce.6.cloned.1.call-update) | async-done | bytes 68171792
  (598 shorter events, 295.5 us)
Async XLA Ops:
  7.2 331.9 %all-gather.11.cloned.1.call-start = ((), (), s32[]{:S(2)}) async-start(), calls=%async_computation.1 | async-start | bytes 2162688 | tf_op jit(solution)/shard_map/all_gather | solution.py:72
  7.9 331.2 %all-gather.15.cloned.1.call-start = ((), (), s32[]{:S(2)}) async-start(), calls=%async_computation.3 | async-start | bytes 2162688 | tf_op jit(solution)/shard_map/all_gather | solution.py:73
  8.7 330.5 %all-gather.17.cloned.1.call-start = ((), (), s32[]{:S(2)}) async-start(), calls=%async_computation.4 | async-start | bytes 2162688 | tf_op jit(solution)/shard_map/all_gather | solution.py:75
  9.4 329.7 %all-gather.13.cloned.1.call-start = ((), (), s32[]{:S(2)}) async-start(), calls=%async_computation.2 | async-start | bytes 4325376 | tf_op jit(solution)/shard_map/all_gather | solution.py:74
  10.0 329.2 %all-gather.21.cloned.1.call-start = ((), (), s32[]{:S(2)}) async-start(), calls=%async_computation.6 | async-start | bytes 5947392 | tf_op jit(solution)/shard_map/all_gather | solution.py:77
  10.6 379.3 %all-gather.9.cloned.1.call-start = ((), (), s32[]{:S(2)}) async-start(), calls=%async_computation | async-start | bytes 6488064 | tf_op jit(solution)/shard_map/all_gather | solution.py:71
  11.2 471.3 %all-gather.19.cloned.1.call-start = ((), (), s32[]{:S(2)}) async-start(), calls=%async_computation.5 | async-start | bytes 11894784 | tf_op jit(solution)/shard_map/all_gather | solution.py:76
  11.9 1985.0 %all-reduce.6.cloned.1.call-start = ((), (), s32[]{:S(2)}) async-start(), calls=%async_computation.7 | async-start | bytes 136347648
  294.2 188.3 %copy-start.38 = (bf16[2,192,1024]{2,1,0:T(8,128)(2,1)S(1)}, bf16[2,192,1024]{2,1,0:T(8,128)(2,1)}, u32[]{:S(2)}) copy-start(bf16[2,192,1024]{2,1,0:T(8,128)(2,1)} %param.17) | copy-start | bytes 2359300
  294.2 188.3 %copy-start.81 = (s32[2]{0:T(128)S(1)}, s32[2]{0:T(128)}, u32[]{:S(2)}) copy-start(s32[2]{0:T(128)} %param.21) | copy-start | bytes 28
  520.3 29.0 %copy-start.8 = (f32[192,1024]{1,0:T(8,128)}, f32[192,1024]{1,0:T(8,128)S(1)}, u32[]{:S(2)}) copy-start(f32[192,1024]{1,0:T(8,128)S(1)} %get-tuple-element.819) | copy-start | bytes 2359300 | tf_op jit(solution)/shard_map/while
  578.2 12.0 copy-start.58
  680.0 18.7 copy-start.8
  727.7 16.2 copy-start.58
  727.7 16.2 copy-start.51
  727.7 16.2 copy-start.71
  747.9 15.2 slice-start.2
  749.3 13.8 slice-start.3
  749.3 13.8 slice-start.4
  888.6 21.8 %slice-start.10 = ((s8[23068672]{0:T(1024)(128)(4,1)}), s8[2097152]{0:T(1024)(128)(4,1)S(1)}, s32[]{:S(2)}) async-start(s8[23068672]{0:T(1024)(128)(4,1)} %bitcast.383), calls=%async_computation.18 | async-start | bytes 4194304
  888.6 21.8 %slice-start.11 = ((s8[23068672]{0:T(1024)(128)(4,1)}), s8[4194304]{0:T(1024)(128)(4,1)S(1)}, s32[]{:S(2)}) async-start(s8[23068672]{0:T(1024)(128)(4,1)} %bitcast.383), calls=%async_computation.19 | async-start | bytes 8388608
  893.3 17.1 slice-start.12
  897.9 12.5 slice-start.13
  897.9 12.5 slice-start.14
  (175 other events, 730.3 us)
Sparse Core Ops, SparseCore 0:
  10.9 59.0 all-gather.10
  72.9 55.2 all-gather.14
  131.0 55.2 all-gather.16
  189.0 60.8 all-gather.12
  252.6 66.1 all-gather.20
  321.5 68.4 all-gather.8
  392.8 89.6 all-gather.18
  1013.4 983.4 all-reduce.5
where the time goes:
time: 2020 us
  waiting for transfers between devices  1130 us (56%)
  local copies, waits for them, and re-layouts  524 us (26%)
  matrix products  238 us (12%)
  blocking collectives  83 us (4%)
    unnamed x9, waiting for transfers between devices  988 us
    gather x1, local copies, waits for them, and re-layouts, on_device(): bucket_map = jnp.take(bucket_ids, distance).reshape(-1)  229 us
    all_gather x1, waiting for transfers between devices, fetch_forward(): lax.all_gather(ff_in, ('dp', 'fsdp'), axis=0, tiled=True)  92.6 us
    reshape x1, local copies, waits for them, and re-layouts, settle(): jnp.concatenate(pieces, axis=1).reshape(-1)  82.4 us
    reshape x8, local copies, waits for them, and re-layouts, settle(): piece = total.reshape(blocks, -1)  66.5 us
    unnamed x42, local copies, waits for them, and re-layouts  56.6 us
    all_gather x1, waiting for transfers between devices, fetch_forward(): lax.all_gather(self_qkv, ('dp', 'fsdp'), axis=0, tiled=True)  50.7 us
    unnamed x1, blocking collectives  42.9 us
  transfers between devices with their start and end apart: 8, of which 3 were waited for; matrix products, arithmetic and copies ran while one was open for 12% of the time, Pallas kernels for 0%

commit v1 on v0

v1 whole, which is shorter than its diff:
```python
import functools

import jax
import jax.numpy as jnp
from jax import lax
from jax.experimental import pallas as pl
from jax.experimental.pallas import tpu as pltpu
from jax.sharding import PartitionSpec as P

HEADS = 16
HEAD = 64
BUCKETS = 32
PACK = 32
LANES = 128
PIECE = 32 * 1024

MESH = pl.DeviceIdType.MESH


class Place:
    def __init__(self, dp, fsdp):
        self.sizes = (dp // 2, 2, fsdp // 2, 2)

    def locate(self):
        row, column = lax.axis_index("dp"), lax.axis_index("fsdp")
        sizes = self.sizes
        self.here = (row // sizes[1], row % sizes[1], column // sizes[3], column % sizes[3])

    def moved(self, axis, step):
        coords = list(self.here)
        coords[axis] = (coords[axis] + step) % self.sizes[axis]
        return coords

    def device(self, coords):
        return (coords[0] * self.sizes[1] + coords[1], coords[2] * self.sizes[3] + coords[3])

    def peers(self):
        return [(axis, step) for axis in range(4) for step in range(1, self.sizes[axis])]

    def greet(self):
        barrier = pltpu.get_barrier_semaphore()
        for axis, step in self.peers():
            pl.semaphore_signal(
                barrier, inc=1, device_id=self.device(self.moved(axis, step)), device_id_type=MESH
            )
        pl.semaphore_wait(barrier, len(self.peers()))


class Unit:
    def __init__(self, owner, block, start, count):
        self.owner, self.start, self.count = owner, start, count
        self.grouped = len(block) == 3
        self.shape = (count,) + block[1:] if self.grouped else (block[0], count)
        width = self.shape[-1]
        self.halves = 2 if width % 256 == 0 else 1
        self.half = width // self.halves

    def part(self, half=None):
        low, size = (0, self.shape[-1]) if half is None else (half * self.half, self.half)
        if self.grouped:
            return (pl.ds(self.start, self.count), slice(None), pl.ds(low, size))
        return (slice(None), pl.ds(self.start + low, size))

    def local(self, half):
        return (slice(None),) * (len(self.shape) - 1) + (pl.ds(half * self.half, self.half),)

    def half_shape(self):
        return self.shape[:-1] + (self.half,)


def make_units(blocks, piece):
    units = []
    for owner, block in enumerate(blocks):
        total, most = (block[0], piece // 8 // block[2] or 1) if len(block) == 3 else (block[1], piece // block[0])
        start = 0
        while start < total:
            count = min(most, total - start)
            units.append(Unit(owner, block, start, count))
            start += count
    return units


def gather_kernel(place, units, count, *refs):
    shards, wholes = refs[:count], refs[count : 2 * count]
    send_sems, recv_sems, local_sems = refs[2 * count :]
    place.locate()
    place.greet()
    zi, yi, xi, ci = place.here
    sizes = place.sizes
    started = []
    serial = [0]

    def send(source, target, axis, step):
        spot = serial[0]
        serial[0] += 1
        copy = pltpu.make_async_remote_copy(
            src_ref=source,
            dst_ref=target,
            send_sem=send_sems.at[spot],
            recv_sem=recv_sems.at[spot],
            device_id=place.device(place.moved(axis, step)),
            device_id_type=MESH,
        )
        copy.start()
        started.append(copy)
        return copy

    pending = {}

    def along(axis, source, target):
        return [send(source, target, axis, step) for step in range(1, sizes[axis])]

    def first(u):
        unit = units[u]
        shard = shards[unit.owner].at[unit.part()]
        own = wholes[unit.owner].at[(zi, yi, xi, ci) + unit.part()]
        copy = pltpu.make_async_copy(shard, own, local_sems.at[u])
        copy.start()
        pending[u] = (copy, along(0, shard, own))

    def settle(u):
        for copy in pending[u]:
            copy.wait_recv()

    def second(u):
        copy, others = pending[u]
        copy.wait()
        for other in others:
            other.wait_recv()
        unit = units[u]
        whole = wholes[unit.owner]
        pending[u] = []
        for half in range(unit.halves):
            ref = whole.at[(slice(None), yi, xi, ci) + unit.part(half)]
            pending[u] += along(2 - half, ref, ref)

    def third(u):
        settle(u)
        unit = units[u]
        whole = wholes[unit.owner]
        pending[u] = []
        for half in range(unit.halves):
            index = (slice(None), yi, slice(None), ci) if half == 0 else (slice(None), slice(None), xi, ci)
            ref = whole.at[index + unit.part(half)]
            pending[u] += along(1 + half, ref, ref)

    def fourth(u):
        settle(u)
        unit = units[u]
        ref = wholes[unit.owner].at[(slice(None), slice(None), slice(None), ci) + unit.part()]
        pending[u] = along(3, ref, ref)

    stages = (first, second, third, fourth, settle)
    for tick in range(len(units) + len(stages) - 1):
        for lag, stage in enumerate(stages):
            if 0 <= tick - lag < len(units):
                stage(tick - lag)
    for copy in started:
        copy.wait_send()


def scatter_kernel(place, units, count, slot_of, *refs):
    wholes, owned = refs[:count], refs[count : 2 * count]
    refs = refs[2 * count :]
    scratch = [refs[6 * u : 6 * u + 6] for u in range(len(units))]
    slots = refs[6 * len(units) : -3]
    send_sems, recv_sems, local_sems = refs[-3:]
    place.locate()
    place.greet()
    zi, yi, xi, ci = place.here
    sizes = place.sizes
    full = slice(None)
    started, serial, pending = [], [0], {}

    def send(source, target, axis, step):
        spot = serial[0]
        serial[0] += 1
        copy = pltpu.make_async_remote_copy(
            src_ref=source,
            dst_ref=target,
            send_sem=send_sems.at[spot],
            recv_sem=recv_sems.at[spot],
            device_id=place.device(place.moved(axis, step)),
            device_id_type=MESH,
        )
        copy.start()
        started.append(copy)
        return copy

    def settle(u):
        for copy in pending[u]:
            copy.wait_recv()
        pending[u] = []

    def add(total, target, terms, kind=jnp.bfloat16):
        def body(spot, carry):
            value = sum(term(spot).astype(jnp.float32) for term in terms)
            ref, index = target(spot)
            ref[index] = value.astype(kind)
            return carry

        lax.fori_loop(0, total, body, 0)

    def slot(u):
        kind, place_in = slot_of[u]
        return slots[kind].at[place_in]

    def first(u):
        unit = units[u]
        whole = wholes[unit.owner]
        arrived = scratch[u][0]
        mine = pltpu.make_async_copy(
            whole.at[(full, full, full, ci) + unit.part()], slot(u), local_sems.at[u]
        )
        mine.start()
        theirs = send(
            whole.at[(full, full, full, (ci + 1) % 2) + unit.part()], arrived, 3, 1
        )
        pending[u] = (mine, theirs)

    def second(u):
        unit = units[u]
        arrived, one_a, one_b = scratch[u][:3]
        own = slot(u)
        mine, theirs = pending[u]
        mine.wait()
        theirs.wait_recv()
        flat = lambda b: (b // (sizes[1] * sizes[2]), (b // sizes[2]) % sizes[1], b % sizes[2])
        add(
            sizes[0] * sizes[1] * sizes[2],
            lambda b: (arrived, flat(b)),
            [lambda b: arrived[flat(b)], lambda b: own[flat(b)]],
        )
        pending[u] = []
        for half in range(unit.halves):
            axis, target = (1, one_a) if half == 0 else (2, one_b)
            for step in range(1, sizes[axis]):
                there = place.moved(axis, step)[axis]
                index = (full, there, full) if half == 0 else (full, full, there)
                pending[u].append(
                    send(arrived.at[index + unit.local(half)], target.at[step - 1], axis, step)
                )

    def third(u):
        settle(u)
        unit = units[u]
        arrived, one_a, one_b, two_a, two_b = scratch[u][:5]
        for half in range(unit.halves):
            axis, other = (1, 2) if half == 0 else (2, 1)
            one, two = (one_a, two_a) if half == 0 else (one_b, two_b)
            wide = sizes[other]

            def mine(b, half=half, wide=wide):
                middle = (yi, b % wide) if half == 0 else (b % wide, xi)
                return arrived[(b // wide,) + middle + unit.local(half)]

            add(
                sizes[0] * wide,
                lambda b: (one, (0, b // wide, b % wide)),
                [mine]
                + [
                    lambda b, step=step: one[step, b // wide, b % wide]
                    for step in range(sizes[axis] - 1)
                ],
            )
            for step in range(1, wide):
                there = place.moved(other, step)[other]
                pending[u].append(send(one.at[0, :, there], two.at[step - 1], other, step))

    def fourth(u):
        settle(u)
        unit = units[u]
        one_a, one_b, two_a, two_b, last = scratch[u][1:]
        for half in range(unit.halves):
            axis, here = (2, xi) if half == 0 else (1, yi)
            one, two = (one_a, two_a) if half == 0 else (one_b, two_b)
            add(
                sizes[0],
                lambda b: (two, (0, b)),
                [lambda b: one[0, b, here]]
                + [lambda b, step=step: two[step, b] for step in range(sizes[axis] - 1)],
            )
            for step in range(1, sizes[0]):
                there = place.moved(0, step)[0]
                pending[u].append(
                    send(two.at[0, there], last.at[(step - 1,) + unit.local(half)], 0, step)
                )

    def fifth(u):
        settle(u)
        unit = units[u]
        two_a, two_b, last = scratch[u][3:]
        for half in range(unit.halves):
            two = two_a if half == 0 else two_b
            value = two[0, zi].astype(jnp.float32)
            for step in range(sizes[0] - 1):
                value = value + last[(step,) + unit.local(half)].astype(jnp.float32)
            owned[unit.owner][unit.part(half)] = value

    stages = (first, second, third, fourth, fifth)
    for tick in range(len(units) + len(stages) - 1):
        for lag, stage in enumerate(stages):
            if 0 <= tick - lag < len(units):
                stage(tick - lag)
    for copy in started:
        copy.wait_send()


def copies_of(units, sizes, per_z):
    total = 0
    for unit in units:
        total += (sizes[0] - 1) * (unit.halves if per_z else 1) + 1
        total += unit.halves * (sizes[1] - 1 + sizes[2] - 1)
    return total


def gather_all(place, blocks, shards):
    units = make_units(blocks, PIECE)
    total = copies_of(units, place.sizes, False)
    anywhere = pl.BlockSpec(memory_space=pl.ANY)
    return pl.pallas_call(
        functools.partial(gather_kernel, place, units, len(blocks)),
        out_shape=[jax.ShapeDtypeStruct(place.sizes + block, jnp.bfloat16) for block in blocks],
        in_specs=[anywhere] * len(blocks),
        out_specs=[anywhere] * len(blocks),
        scratch_shapes=[
            pltpu.SemaphoreType.DMA((total,)),
            pltpu.SemaphoreType.DMA((total,)),
            pltpu.SemaphoreType.DMA((len(units),)),
        ],
        compiler_params=pltpu.CompilerParams(collective_id=0, has_side_effects=True),
        name="gather_all",
    )(*shards)


def scatter_all(place, blocks, wholes):
    units = make_units(blocks, PIECE)
    sizes = place.sizes
    total = copies_of(units, sizes, True)
    scratch, kinds, slot_of = [], [], []
    seen = {}
    for unit in units:
        half = unit.half_shape()
        for shape in (
            sizes[:3] + unit.shape,
            (sizes[1] - 1, sizes[0], sizes[2]) + half,
            (sizes[2] - 1, sizes[0], sizes[1]) + half,
            (sizes[2] - 1, sizes[0]) + half,
            (sizes[1] - 1, sizes[0]) + half,
            (sizes[0] - 1,) + unit.shape,
        ):
            scratch.append(pltpu.VMEM(shape, jnp.bfloat16))
        if unit.shape not in seen:
            seen[unit.shape] = [len(kinds), 0]
            kinds.append(pltpu.VMEM((3,) + sizes[:3] + unit.shape, jnp.bfloat16))
        kind = seen[unit.shape]
        slot_of.append((kind[0], kind[1] % 3))
        kind[1] += 1
    anywhere = pl.BlockSpec(memory_space=pl.ANY)
    return pl.pallas_call(
        functools.partial(scatter_kernel, place, units, len(blocks), slot_of),
        out_shape=[jax.ShapeDtypeStruct(block, jnp.float32) for block in blocks],
        in_specs=[anywhere] * len(blocks),
        out_specs=[pl.BlockSpec(memory_space=pltpu.VMEM)] * len(blocks),
        scratch_shapes=scratch
        + kinds
        + [
            pltpu.SemaphoreType.DMA((total,)),
            pltpu.SemaphoreType.DMA((total,)),
            pltpu.SemaphoreType.DMA((len(units),)),
        ],
        compiler_params=pltpu.CompilerParams(
            collective_id=1, has_side_effects=True, vmem_limit_bytes=60 * 2**20
        ),
        name="scatter_all",
    )(*wholes)


def norm_scale(stream, gain):
    return stream * lax.rsqrt(jnp.mean(stream * stream, axis=-1, keepdims=True) + 1e-06) * gain


def gelu_tanh(values):
    return (
        0.5
        * values
        * (1.0 + jnp.tanh(0.7978845608028654 * (values + 0.044715 * values * values * values)))
    )


def gated(gate_up):
    half_width = gate_up.shape[1] // 2
    return gelu_tanh(gate_up[:, :half_width]) * gate_up[:, half_width:]


def product(spec, left, right):
    return jnp.einsum(spec, left, right, preferred_element_type=jnp.float32)


def attend(queries, key_rows, value_rows, pos_bias, keep_mask):
    scores = product("bihc,bjhc->bhij", queries, key_rows) * HEAD ** (-0.5)
    if pos_bias is not None:
        scores = scores + pos_bias
    masked = jnp.where(keep_mask[:, None], scores, -1e30)
    row_max = jnp.max(masked, axis=-1, keepdims=True)
    powers = jnp.exp(masked - row_max)
    probs = powers / jnp.sum(powers, axis=-1, keepdims=True)
    low_probs = probs.astype(jnp.bfloat16)
    mixed = product("bhij,bjhc->bihc", low_probs, value_rows)
    return mixed.astype(jnp.bfloat16), low_probs


def attend_back(queries, key_rows, value_rows, low_probs, grad_mixed):
    probs = low_probs.astype(jnp.float32)
    grad_values = product("bhij,bihc->bjhc", low_probs, grad_mixed)
    grad_probs = product("bihc,bjhc->bhij", grad_mixed, value_rows)
    grad_scores = (
        probs * (grad_probs - jnp.sum(probs * grad_probs, axis=-1, keepdims=True))
    ).astype(jnp.bfloat16)
    grad_queries = product("bhij,bjhc->bihc", grad_scores, key_rows) * HEAD ** (-0.5)
    grad_keys = product("bhij,bihc->bjhc", grad_scores, queries) * HEAD ** (-0.5)
    return grad_queries, grad_keys, grad_values, grad_scores


def toeplitz(table, size):
    lead = table.shape[:-1]
    row = jnp.concatenate(
        [table[..., ::-1], jnp.broadcast_to(table[..., :1], lead + (size,))], axis=-1
    )
    tiled = jnp.broadcast_to(row[..., None, :], lead + (size, 2 * size)).reshape(lead + (-1,))
    tiled = jnp.concatenate([tiled[..., size - 1 :], row[..., :1]], axis=-1)
    tiled = tiled[..., : size * (2 * size - 1)]
    return tiled.reshape(lead + (size, 2 * size - 1))[..., :size]


def layer(weights, gains, rel_bias, tokens, encoder, cotangent, lengths, enc_lengths, bucket_ids):
    self_qkv, self_out, cross_q, cross_kv, cross_out, ff_in, ff_out = weights
    count, slots, width = tokens.shape
    enc_count = encoder.shape[1]
    bucket_map = toeplitz(bucket_ids, slots).reshape(-1)
    onehot = (lax.iota(jnp.int32, BUCKETS)[:, None] == bucket_map[None, :]).astype(jnp.bfloat16)
    pos_bias = jnp.dot(rel_bias, onehot, preferred_element_type=jnp.float32).reshape(
        HEADS, slots, slots
    )
    row_ids = lax.iota(jnp.int32, slots)
    self_mask = (row_ids[None, None, :] <= row_ids[None, :, None]) & (
        row_ids[None, None, :] < lengths[:, None, None]
    )
    cross_mask = lax.iota(jnp.int32, enc_count)[None, None, :] < enc_lengths[:, None, None]
    enc_rows = encoder.reshape(count * enc_count, width)
    dot = functools.partial(jnp.dot, preferred_element_type=jnp.float32)
    low = lambda value: value.astype(jnp.bfloat16)
    stream = tokens.reshape(count * slots, width).astype(jnp.float32)
    normed_self, back_self = jax.vjp(norm_scale, stream, gains[0])
    normed_self = low(normed_self)
    qkv = low(dot(normed_self, self_qkv)).reshape(count, slots, 3, HEADS, HEAD)
    mixed_self, probs_self = attend(qkv[:, :, 0], qkv[:, :, 1], qkv[:, :, 2], pos_bias, self_mask)
    mixed_self = mixed_self.reshape(count * slots, width)
    second = stream + dot(mixed_self, self_out)
    normed_cross, back_cross = jax.vjp(norm_scale, second, gains[1])
    normed_cross = low(normed_cross)
    queries = low(dot(normed_cross, cross_q)).reshape(count, slots, HEADS, HEAD)
    pairs = low(dot(enc_rows, cross_kv)).reshape(count, enc_count, 2, HEADS, HEAD)
    mixed_cross, probs_cross = attend(queries, pairs[:, :, 0], pairs[:, :, 1], None, cross_mask)
    mixed_cross = mixed_cross.reshape(count * slots, width)
    third = second + dot(mixed_cross, cross_out)
    normed_ffn, back_ffn = jax.vjp(norm_scale, third, gains[2])
    normed_ffn = low(normed_ffn)
    gate_up = dot(normed_ffn, ff_in)
    activated, back_gate = jax.vjp(gated, gate_up)
    hidden = low(activated)
    outcome = third + dot(hidden, ff_out)

    valid = (row_ids[None, :] < lengths[:, None]).astype(jnp.float32)[:, :, None]
    grad_out = (cotangent.astype(jnp.float32) * valid).reshape(count * slots, width)
    branch = low(grad_out)
    grad_ff_out = product("lf,ld->fd", hidden, branch)
    grad_hidden = product("ld,fd->lf", branch, ff_out)
    (grad_gate_up,) = back_gate(grad_hidden)
    grad_gate_up = low(grad_gate_up)
    grad_ff_in = product("ld,lf->df", normed_ffn, grad_gate_up)
    grad_stream, gain_ffn = back_ffn(product("lf,df->ld", grad_gate_up, ff_in))
    grad_third = grad_out + grad_stream
    branch = low(grad_third)
    grad_cross_out = product("le,ld->ed", mixed_cross, branch)
    grad_mixed = low(product("ld,ed->le", branch, cross_out)).reshape(count, slots, HEADS, HEAD)
    grad_queries, grad_keys, grad_values, unused = attend_back(
        queries, pairs[:, :, 0], pairs[:, :, 1], probs_cross, grad_mixed
    )
    grad_query_rows = low(grad_queries.reshape(count * slots, width))
    grad_pair_rows = low(
        jnp.concatenate(
            [
                grad_keys.reshape(count * enc_count, width),
                grad_values.reshape(count * enc_count, width),
            ],
            axis=1,
        )
    )
    grad_cross_q = product("ld,le->de", normed_cross, grad_query_rows)
    grad_cross_kv = product("ed,ef->df", enc_rows, grad_pair_rows)
    grad_enc = product("ef,df->ed", grad_pair_rows, cross_kv)
    grad_stream, gain_cross = back_cross(product("le,de->ld", grad_query_rows, cross_q))
    grad_second = grad_third + grad_stream
    branch = low(grad_second)
    grad_self_out = product("le,ld->ed", mixed_self, branch)
    grad_mixed = low(product("ld,ed->le", branch, self_out)).reshape(count, slots, HEADS, HEAD)
    grad_queries, grad_keys, grad_values, grad_scores = attend_back(
        qkv[:, :, 0], qkv[:, :, 1], qkv[:, :, 2], probs_self, grad_mixed
    )
    score_sums = jnp.sum(grad_scores.astype(jnp.float32), axis=0).reshape(HEADS, slots * slots)
    grad_rel_bias = product("hn,bn->hb", low(score_sums), onehot)
    grad_qkv = low(
        jnp.concatenate(
            [part.reshape(count * slots, width) for part in (grad_queries, grad_keys, grad_values)],
            axis=1,
        )
    )
    grad_self_qkv = product("ld,lf->df", normed_self, grad_qkv)
    grad_stream, gain_self = back_self(product("lf,df->ld", grad_qkv, self_qkv))
    grad_tok = grad_second + grad_stream
    grad_gains = jnp.stack([gain_self, gain_cross, gain_ffn], axis=0)
    grads = (
        grad_self_qkv,
        grad_self_out,
        grad_cross_q,
        grad_cross_kv,
        grad_cross_out,
        grad_ff_in,
        grad_ff_out,
    )
    return (
        outcome.reshape(tokens.shape),
        grad_tok.reshape(tokens.shape),
        grad_enc.reshape(encoder.shape),
        grads,
        grad_gains,
        grad_rel_bias,
    )


AXES = ("dp", "fsdp")


def by_collectives(data, shards):
    whole = lambda shard, axis=0: lax.all_gather(shard, AXES, axis=axis, tiled=True)
    weights = tuple(whole(shard) for shard in shards[:7])
    gains = whole(shards[7], 1).astype(jnp.float32)
    rel_bias = whole(shards[8]).reshape(HEADS, BUCKETS)
    outcome, grad_tok, grad_enc, grads, grad_gains, grad_rel_bias = layer(
        weights, gains, rel_bias, *data
    )
    settle = lambda total, axis=0: lax.psum_scatter(
        total, AXES, scatter_dimension=axis, tiled=True
    )
    return (
        (outcome, grad_tok, grad_enc)
        + tuple(settle(grad) for grad in grads)
        + (settle(grad_gains, 1), settle(grad_rel_bias.reshape(-1)))
    )


def by_kernels(place, data, shards):
    norm_gains, rel_bias = shards[7:]
    count = place.sizes[0] * place.sizes[1] * place.sizes[2] * place.sizes[3]
    me = lax.axis_index(AXES)
    norms, per = norm_gains.shape
    group = LANES // per
    rel_per = rel_bias.shape[0]
    pack = jnp.zeros((PACK, LANES), jnp.bfloat16)
    pack = lax.dynamic_update_slice(pack, norm_gains, (0, (me % group) * per))
    rel_row, rel_column = HEADS + me * rel_per // BUCKETS, (me * rel_per) % BUCKETS
    pack = lax.dynamic_update_slice(pack, rel_bias.reshape(1, rel_per), (rel_row, rel_column))
    ff_rows, width = shards[6].shape
    ff_shape = (ff_rows // 8, 8, width)
    sent = (pack,) + shards[:6] + (shards[6].reshape(ff_shape),)
    blocks = [piece.shape for piece in sent]
    packs, *wholes = gather_all(place, blocks, sent)
    weights = tuple(
        whole.reshape(count * shard.shape[0], shard.shape[1])
        for whole, shard in zip(wholes, shards[:7])
    )
    packs = packs.reshape(count // group, group, PACK, LANES).astype(jnp.float32).sum(axis=1)
    gains = packs[:, :norms].transpose(1, 0, 2).reshape(norms, -1)
    rel_table = packs.sum(axis=0)[HEADS:, :BUCKETS].astype(jnp.bfloat16)
    outcome, grad_tok, grad_enc, grads, grad_gains, grad_rel_bias = layer(
        weights, gains, rel_table, *data
    )
    top = grad_gains.reshape(norms, count // group, LANES).transpose(1, 0, 2)
    top = jnp.pad(top, ((0, 0), (0, HEADS - norms), (0, 0)))
    low_part = jnp.pad(grad_rel_bias, ((0, 0), (0, LANES - BUCKETS)))
    low_part = jnp.broadcast_to(low_part, (count // group, HEADS, LANES))
    tiles = jnp.concatenate([top, low_part], axis=1)[:, None]
    tiles = jnp.broadcast_to(tiles, (count // group, group, PACK, LANES))
    sums = scatter_all(
        place,
        blocks,
        [
            piece.astype(jnp.bfloat16).reshape(place.sizes + block)
            for piece, block in zip((tiles,) + grads, blocks)
        ],
    )
    packed, *owned = sums
    own_gains = lax.dynamic_slice(packed, (0, (me % group) * per), (norms, per))
    own_rel = lax.dynamic_slice(packed, (rel_row, rel_column), (1, rel_per)).reshape(-1)
    owned[6] = owned[6].reshape(ff_rows, width)
    return (outcome, grad_tok, grad_enc) + tuple(owned) + (own_gains, own_rel)


def on_device(place, *args):
    data, shards = args[:6], args[6:]
    per = shards[7].shape[1]
    regular = all(shard.shape[0] % 16 == 0 for shard in shards[:6])
    if regular and shards[6].shape[0] % 8 == 0 and LANES % per == 0:
        return by_kernels(place, data, shards)
    return by_collectives(data, shards)


def solution(mesh):
    rows = P(AXES, None, None)
    flat = P(AXES)
    matrix = P(AXES, None)
    split = P(None, AXES)
    place = Place(mesh.shape["dp"], mesh.shape["fsdp"])
    return jax.shard_map(
        functools.partial(on_device, place),
        mesh=mesh,
        in_specs=(rows, rows, rows, flat, flat, P()) + (matrix,) * 7 + (split, flat),
        out_specs=(rows, rows, rows) + (matrix,) * 7 + (split, flat),
        check_vma=False,
    )
```

time: 2020 us -> 666 us (0.33)
  waiting for transfers between devices: 1130 us -> 0 us
  local copies, waits for them, and re-layouts: 524 us -> 130 us
  Pallas kernels: 0 us -> 322 us
  blocking collectives: 83 us -> 0 us
  matrix products: 238 us -> 161 us
  other arithmetic: 18.2 us -> 41.7 us
    unnamed x9 -> x0, waiting for transfers between devices: 988 us -> none
    pallas_call x0 -> x2, Pallas kernels: none -> 322 us  [the longest x1 163 us: scatter_all(): pl.pallas_call(functools.partial(scatter_kernel, place, units, len(blocks...]
    gather x1 -> x0, local copies, waits for them, and re-layouts: 229 us -> none  [on_device(): bucket_map = jnp.take(bucket_ids, distance).reshape(-1)]
    all_gather x7 -> x0, waiting for transfers between devices: 143 us -> none  [the longest x1 92.6 us: fetch_forward(): lax.all_gather(ff_in, ('dp', 'fsdp'), axis=0, tiled=True)]
    reshape x25 -> x16, local copies, waits for them, and re-layouts: 162 us -> 48.5 us  [the longest x3 9.35 us: layer(): part.reshape(count * slots, width)]
    dot_general x69 -> x35, matrix products: 238 us -> 161 us  [the longest x27 124 us: product(): return jnp.einsum(spec, left, right, preferred_element_type=jnp.float32)]
    unnamed x1 -> x0, blocking collectives: 42.9 us -> none
    while x352 -> x0, local copies, waits for them, and re-layouts: 40.1 us -> none
  transfers between devices with their start and end apart: 8 -> 0, of which waited for: 3 -> 0; matrix products, arithmetic and copies ran while one was open for 12% -> 0% of each run, Pallas kernels for 0% -> 0%
where the time goes in v1:
time: 666 us; the launch traced here: 657 us
  Pallas kernels  322 us (48%)
  matrix products  161 us (24%)
  local copies, waits for them, and re-layouts  130 us (20%)
  other arithmetic  41.7 us (6%)
    pallas_call x1, Pallas kernels, scatter_all(): pl.pallas_call(functools.partial(scatter_kernel, place, units, len(blocks...  163 us
    pallas_call x1, Pallas kernels, gather_all(): pl.pallas_call(functools.partial(gather_kernel, place, units, len(blocks)...  159 us
    dot_general x27, matrix products, product(): return jnp.einsum(spec, left, right, preferred_element_type=jnp.float32)  124 us
    unnamed x136, local copies, waits for them, and re-layouts  26.2 us
    sub x2, other arithmetic, attend(): powers = jnp.exp(masked - row_max)  19.7 us

profile of v1, /device:TPU:0, one launch (start us, length us, event | category | flops | bytes accessed | tf_op | source)
XLA Modules:
  0.0 656.7 jit_solution(5211158678889808861)
XLA Ops:
  3.8 159.1 %gather_all.1 = (bf16[4,2,2,2,32,128]{5,4,3,2,1,0:T(8,128)(2,1)}, bf16[4,2,2,2,32,3072]{5,4,3,2,1,0:T(8,128)(2,1)}, bf16[4,2,2,2,32,1024]{5,4,3,2,1,0:T(8,128)(2...) custom-call(bf16[32,128]{1,0:T(8,128)(2,1)} %copy-done.41, ...), custom_call_target="tpu_custom_call" | custom-call | tf_op jit(solution)/shard_map/gather_all/pallas_call | solution.py:321
  165.6 6.6 %convolution_convert_fusion.3 = bf16[384,3072]{1,0:T(8,128)(2,1)} fusion(bf16[384,1024]{1,0:T(8,128)(2,1)S(1)} %bitcast.214, bf16[1024,3072]{1,0:T(8,128)(2,1)} %bitcast.238), kind=kOutput, calls=%fused_computation.37 | convolution fusion | flops 2417098752 | bytes 9437184 | tf_op jit(solution)/shard_map/dot_general | solution.py:456
  172.2 6.8 %reshape.379 = bf16[2,192,3,16,64]{4,3,2,1,0:T(8,128)(2,1)} reshape(bf16[384,3072]{1,0:T(8,128)(2,1)} %convolution_convert_fusion.3) | data formatting | bytes 4718592 | tf_op jit(solution)/shard_map/reshape | solution.py:456
  179.0 4.9 fusion.82
  188.5 5.3 fusion.53
  206.3 9.9 %fusion.85 = (f32[2,16,192]{2,1,0:T(8,128)S(1)}, f32[2,16,192,192]{2,3,1,0:T(8,128)S(1)}) fusion(f32[2,16,192,192]{2,3,1,0:T(8,128)} %fusion.53, f32[16,192,192]{1,2,0:T(8,128)} %copy.111, pred[2,192,192]{1,2,0:T(8,128)(4,1)S(1)} %broadcast_and_fusion), kind=kOutput, calls=%fused_computation.168 | output fusion | flops 9437375 | bytes 11894784 | tf_op jit(solution)/shard_map/sub | solution.py:406
  242.6 7.5 %fusion.29 = bf16[768,2048]{0,1:T(8,128)(2,1)} fusion(bf16[1024,2048]{1,0:T(8,128)(2,1)} %bitcast.244, bf16[768,1024]{1,0:T(8,128)(2,1)S(1)} %bitcast.188), kind=kOutput, calls=%fused_computation.54 | convolution fusion | flops 3222798336 | bytes 8912896 | tf_op jit(solution)/shard_map/dot_general | solution.py:463
  250.1 7.0 %reshape.351 = bf16[2,384,2,16,64]{1,0,4,3,2:T(2,128)(2,1)} reshape(bf16[768,2048]{0,1:T(8,128)(2,1)} %fusion.29) | data formatting | bytes 6291456 | tf_op jit(solution)/shard_map/reshape | solution.py:463
  257.1 4.2 fusion.83
  261.4 5.0 fusion.45
  266.4 9.8 %fusion.86 = (f32[2,16,192]{2,1,0:T(8,128)S(1)}, f32[2,16,192,384]{3,2,1,0:T(8,128)S(1)}) fusion(f32[2,16,192,384]{3,2,1,0:T(8,128)} %fusion.45, pred[2,384]{1,0:T(4,128)(4,1)S(1)} %iota_compare_fusion.4), kind=kOutput, calls=%fused_computation.169 | output fusion | flops 14156159 | bytes 18899712 | tf_op jit(solution)/shard_map/sub | solution.py:406
  290.7 8.2 %fusion.79 = f32[384,5632]{1,0:T(8,128)S(1)} fusion(bf16[1024,5632]{1,0:T(8,128)(2,1)} %bitcast.236, f32[384,1024]{1,0:T(8,128)S(1)} %get-tuple-element.77, f32[1024]{0:T(1024)S(1)} %bitcast.227, f32[384]{0:T(512)S(1)} %fusion.68), kind=kOutput, calls=%fused_computation.163 | convolution fusion | flops 4430364672 | bytes 21763584 | tf_op jit(solution)/shard_map/dot_general | solution.py:469
  299.2 8.7 %fusion.43 = (f32[384,2816]{1,0:T(8,128)}, f32[384,2816]{1,0:T(8,128)}, bf16[384,2816]{1,0:T(8,128)(2,1)S(1)}) fusion(f32[384,5632]{1,0:T(8,128)S(1)} %fusion.79, bf16[384,1024]{1,0:T(8,128)(2,1)S(1)} %bitcast.215, bf16[2816,1024]{1,0:T(8,128)(2,1)S(1)} %bitcast.242), kind=kOutput, calls=%fused_computation.96 | convolution fusion | flops 2244870144 | bytes 26017792 | tf_op jit(solution)/shard_map/ld,fd->lf/dot_general | solution.py:397
  311.5 13.1 %multiply_reduce_fusion = (bf16[1024]{0:T(1024)(128)(2,1)S(1)}, f32[384]{0:T(512)S(1)}, f32[384,1024]{1,0:T(8,128)}) fusion(f32[384,1024]{1,0:T(8,128)} %copy-done.30, f32[384]{0:T(512)S(1)} %fusion.68, f32[1024]{0:T(1024)S(1)} %bitcast.228, bf16[1024,5632]{1,0:T(8,128)(2,1)} %bitcast.237, f32[384,2816]{1,0:T(8,128)} %get-tuple-element.53, ...), kind=kOutput, calls=%fused_computation.87 | convolution fusion | flops 4435868160 | bytes 23340032 | tf_op jit(solution)/shard_map/lf,df->ld/dot_general | solution.py:397
  334.5 5.4 fusion.2
  355.3 4.0 convolution_convert_fusion.13
  367.9 6.3 fusion.80
  402.6 7.5 %fusion.37 = (bf16[1024]{0:T(1024)(128)(2,1)S(1)}, f32[384]{0:T(512)S(1)}, bf16[384,1024]{1,0:T(8,128)(2,1)}, f32[384,1024]{1,0:T(8,128)S(1)}) fusion(bf16[2,192,1024]{2,1,0:T(8,128)(2,1)S(1)} %copy-done.21, f32[384]{0:T(512)S(1)} %rsqrt.36, f32[1024]{0:T(1024)S(1)} %bitcast.225, bf16[384,3072]{0,1:T(8,128)(2,1)} %constant_dynamic-update-slice_fusion, ...), kind=kOutput, calls=%fused_computation.81 | convolution fusion | flops 2419456512 | bytes 11805696 | tf_op jit(solution)/shard_map/lf,df->ld/dot_general | solution.py:397
  422.8 8.3 %fusion.18 = f32[2,384,1024]{2,1,0:T(8,128)} fusion(bf16[1024,2048,1]{1,0,2:T(8,128)(2,1)} %bitcast.245, bf16[2,384,1024]{2,1,0:T(8,128)(2,1)} %copy.134, bf16[2,384,1024]{2,1,0:T(8,128)(2,1)} %copy.133), kind=kOutput, calls=%fused_computation.42 | convolution fusion | flops 3227516928 | bytes 10485760 | tf_op jit(solution)/shard_map/ef,df->ed/dot_general | solution.py:397
  440.8 5.5 convolution_convert_fusion.2
  455.7 6.5 convolution_convert_fusion.4
  464.9 9.4 %convolution_convert_fusion = bf16[1024,5632]{1,0:T(8,128)(2,1)} fusion(f32[384,2816]{1,0:T(8,128)S(1)} %bitcast.252, f32[384,2816]{1,0:T(8,128)S(1)} %bitcast.250, f32[384,1024]{1,0:T(8,128)S(1)} %copy-done.31, f32[1024]{0:T(1024)S(1)} %bitcast.230, f32[384]{0:T(512)S(1)} %fusion.68), kind=kOutput, calls=%fused_computation.4 | convolution fusion | flops 4440457216 | bytes 21763584 | tf_op jit(solution)/shard_map/ld,lf->df/dot_general | solution.py:397
  475.9 5.0 convolution_convert_fusion.1
  480.9 163.1 %scatter_all.1 = (f32[32,128]{1,0:T(8,128)}, f32[32,3072]{1,0:T(8,128)}, f32[32,1024]{1,0:T(8,128)}, f32[32,1024]{1,0:T(8,128)}, f32[32,2048]{1,0:T(8,128)}, /*i...) custom-call(bf16[4,2,2,2,32,128]{5,4,3,2,1,0:T(8,128)(2,1)} %broadcast_in_dim.51.refs_0_, ...), custom_call_target="tpu_custom_call" | custom-call | tf_op jit(solution)/shard_map/scatter_all/pallas_call | solution.py:360
  (234 shorter events, 177.7 us)
Async XLA Ops:
  0.6 241.9 %copy-start = (bf16[2,384,1024]{2,1,0:T(8,128)(2,1)S(1)}, bf16[2,384,1024]{2,1,0:T(8,128)(2,1)}, u32[]{:S(2)}) copy-start(bf16[2,384,1024]{2,1,0:T(8,128)(2,1)} %param.16) | copy-start | bytes 4718596
  0.7 164.7 %copy-start.20 = (bf16[2,192,1024]{2,1,0:T(8,128)(2,1)S(1)}, bf16[2,192,1024]{2,1,0:T(8,128)(2,1)}, u32[]{:S(2)}) copy-start(bf16[2,192,1024]{2,1,0:T(8,128)(2,1)} %param.15) | copy-start | bytes 2359300
  233.9 53.7 %copy-start.6 = (f32[384,1024]{1,0:T(8,128)}, f32[384,1024]{1,0:T(8,128)S(1)}, u32[]{:S(2)}) copy-start(f32[384,1024]{1,0:T(8,128)S(1)} %get-tuple-element.73) | copy-start | bytes 4718596
  261.4 18.4 %copy-start.9 = (bf16[2,384,1,16,64]{1,0,4,3,2:T(2,128)(2,1)}, bf16[2,384,1,16,64]{1,0,4,3,2:T(2,128)(2,1)S(1)}, u32[]{:S(2)}) copy-start(bf16[2,384,1,16,64]{1,0,4,3,2:T(2,128)(2,1)S(1)} %get-tuple-element.58) | copy-start | bytes 4718596
  287.6 11.6 %slice-start.5 = ((s8[5767168]{0:T(1024)(128)(4,1)}), s8[4194304]{0:T(1024)(128)(4,1)S(1)}, s32[]{:S(2)}) async-start(s8[5767168]{0:T(1024)(128)(4,1)} %bitcast.240), calls=%async_computation.5 | async-start | bytes 8388608
  290.6 17.3 %copy-start.30 = (f32[384,1024]{1,0:T(8,128)}, f32[384,1024]{1,0:T(8,128)S(1)}, u32[]{:S(2)}) copy-start(f32[384,1024]{1,0:T(8,128)S(1)} %get-tuple-element.77) | copy-start | bytes 4718596
  290.7 8.2 %copy-start.35 = (bf16[2,192,1024]{2,1,0:T(8,128)(2,1)S(1)}, bf16[2,192,1024]{2,1,0:T(8,128)(2,1)}, u32[]{:S(2)}) copy-start(bf16[2,192,1024]{2,1,0:T(8,128)(2,1)} %param.17) | copy-start | bytes 2359300
  290.7 8.5 %slice-start.6 = ((s8[5767168]{0:T(1024)(128)(4,1)}), s8[1572864]{0:T(1024)(128)(4,1)S(1)}, s32[]{:S(2)}) async-start(s8[5767168]{0:T(1024)(128)(4,1)} %bitcast.240), calls=%async_computation.6 | async-start | bytes 3145728
  299.1 25.5 %copy-start.11 = (f32[2,192,1024]{2,1,0:T(8,128)}, f32[2,192,1024]{2,1,0:T(8,128)S(1)}, u32[]{:S(2)}) copy-start(f32[2,192,1024]{2,1,0:T(8,128)S(1)} %get-tuple-element.62) | copy-start | bytes 4718596
  331.3 8.7 %slice-start.2 = ((s8[9437184]{0:T(1024)(128)(4,1)}), s8[1048576]{0:T(1024)(128)(4,1)S(1)}, s32[]{:S(2)}) async-start(s8[9437184]{0:T(1024)(128)(4,1)} %bitcast.192), calls=%async_computation.2 | async-start | bytes 2097152
  394.9 7.7 %copy-start.21 = (bf16[2,192,1024]{2,1,0:T(8,128)(2,1)S(1)}, bf16[2,192,1024]{2,1,0:T(8,128)(2,1)}, u32[]{:S(2)}) copy-start(bf16[2,192,1024]{2,1,0:T(8,128)(2,1)} %param.15) | copy-start | bytes 2359300
  396.9 14.8 %slice-start = ((s8[4718592]{0:T(1024)(128)(4,1)}), s8[524288]{0:T(1024)(128)(4,1)S(1)}, s32[]{:S(2)}) async-start(s8[4718592]{0:T(1024)(128)(4,1)} %bitcast.190), calls=%async_computation | async-start | bytes 1048576
  402.6 7.5 %copy-start.16 = (f32[384,1024]{1,0:T(8,128)S(1)}, f32[384,1024]{1,0:T(8,128)}, u32[]{:S(2)}) copy-start(f32[384,1024]{1,0:T(8,128)} %fusion.33) | copy-start | bytes 4718596
  402.6 9.1 %slice-start.1 = ((s8[4718592]{0:T(1024)(128)(4,1)}), s8[4194304]{0:T(1024)(128)(4,1)S(1)}, s32[]{:S(2)}) async-start(s8[4718592]{0:T(1024)(128)(4,1)} %bitcast.190), calls=%async_computation.1 | async-start | bytes 8388608
  431.1 6.6 %copy-start.38 = (s32[36864]{0:T(1024)S(1)}, s32[36864]{0:T(1024)}, u32[]{:S(2)}) copy-start(s32[36864]{0:T(1024)} %copy-done.37) | copy-start | bytes 442372
  453.7 11.2 %slice-start.7 = ((s8[4325376]{0:T(1024)(128)(4,1)}), s8[4194304]{0:T(1024)(128)(4,1)S(1)}, s32[]{:S(2)}) async-start(s8[4325376]{0:T(1024)(128)(4,1)} %bitcast.249), calls=%async_computation.7 | async-start | bytes 8388608
  453.7 11.2 %slice-start.9 = ((s8[4325376]{0:T(1024)(128)(4,1)}), s8[131072]{0:T(1024)(128)(4,1)S(1)}, s32[]{:S(2)}) async-start(s8[4325376]{0:T(1024)(128)(4,1)} %bitcast.251), calls=%async_computation.9 | async-start | bytes 262144
  455.7 6.6 %copy-start.15 = (f32[384,1024]{1,0:T(8,128)S(1)}, f32[384,1024]{1,0:T(8,128)}, u32[]{:S(2)}) copy-start(f32[384,1024]{1,0:T(8,128)} %copy-done.13) | copy-start | bytes 4718596
  455.7 6.6 %copy-start.29 = (bf16[384,1024]{0,1:T(8,128)(2,1)S(1)}, bf16[384,1024]{0,1:T(8,128)(2,1)}, u32[]{:S(2)}) copy-start(bf16[384,1024]{0,1:T(8,128)(2,1)} %reshape.354) | copy-start | bytes 2359300
  455.7 9.2 %slice-start.8 = ((s8[4325376]{0:T(1024)(128)(4,1)}), s8[131072]{0:T(1024)(128)(4,1)S(1)}, s32[]{:S(2)}) async-start(s8[4325376]{0:T(1024)(128)(4,1)} %bitcast.249), calls=%async_computation.8 | async-start | bytes 262144
  455.7 9.2 %slice-start.10 = ((s8[4325376]{0:T(1024)(128)(4,1)}), s8[4194304]{0:T(1024)(128)(4,1)S(1)}, s32[]{:S(2)}) async-start(s8[4325376]{0:T(1024)(128)(4,1)} %bitcast.251), calls=%async_computation.10 | async-start | bytes 8388608
  464.9 9.4 %copy-start.12 = (f32[2,192,1024]{2,1,0:T(8,128)S(1)}, f32[2,192,1024]{2,1,0:T(8,128)}, u32[]{:S(2)}) copy-start(f32[2,192,1024]{2,1,0:T(8,128)} %copy-done.11) | copy-start | bytes 4718596
  644.0 10.8 %copy-start.36 = (f32[32,5632]{1,0:T(8,128)S(1)}, f32[32,5632]{1,0:T(8,128)}, u32[]{:S(2)}) copy-start(f32[32,5632]{1,0:T(8,128)} %get-tuple-element.105) | copy-start | bytes 2162692
  644.0 11.7 %copy-start.39 = (f32[11,8,1024]{2,1,0:T(8,128)S(1)}, f32[11,8,1024]{2,1,0:T(8,128)}, u32[]{:S(2)}) copy-start(f32[11,8,1024]{2,1,0:T(8,128)} %get-tuple-element.42) | copy-start | bytes 1081348
  (36 other events, 132.3 us)

commit v2 on v1

--- a/solution.py
+++ b/solution.py
@@ -68,9 +68,10 @@
         return self.shape[:-1] + (self.half,)
 
 
-def make_units(blocks, piece):
+def make_units(blocks, piece, order):
     units = []
-    for owner, block in enumerate(blocks):
+    for owner in order:
+        block = blocks[owner]
         total, most = (block[0], piece // 8 // block[2] or 1) if len(block) == 3 else (block[1], piece // block[0])
         start = 0
         while start < total:
@@ -80,35 +81,39 @@
     return units
 
 
-def gather_kernel(place, units, count, *refs):
-    shards, wholes = refs[:count], refs[count : 2 * count]
-    send_sems, recv_sems, local_sems = refs[2 * count :]
-    place.locate()
-    place.greet()
-    zi, yi, xi, ci = place.here
-    sizes = place.sizes
-    started = []
-    serial = [0]
-
-    def send(source, target, axis, step):
-        spot = serial[0]
-        serial[0] += 1
+class Wires:
+    def __init__(self, place, send_sems, recv_sems):
+        self.place, self.send_sems, self.recv_sems = place, send_sems, recv_sems
+        self.started = []
+
+    def send(self, source, target, axis, step):
+        spot = len(self.started)
         copy = pltpu.make_async_remote_copy(
             src_ref=source,
             dst_ref=target,
-            send_sem=send_sems.at[spot],
-            recv_sem=recv_sems.at[spot],
-            device_id=place.device(place.moved(axis, step)),
+            send_sem=self.send_sems.at[spot],
+            recv_sem=self.recv_sems.at[spot],
+            device_id=self.place.device(self.place.moved(axis, step)),
             device_id_type=MESH,
         )
         copy.start()
-        started.append(copy)
+        self.started.append(copy)
         return copy
 
+    def along(self, axis, source, target):
+        return [
+            self.send(source, target, axis, step) for step in range(1, self.place.sizes[axis])
+        ]
+
+    def finish(self):
+        for copy in self.started:
+            copy.wait_send()
+
+
+def gather_stages(place, units, shards, wholes, wires, local_sems):
+    zi, yi, xi, ci = place.here
+    full = slice(None)
     pending = {}
-
-    def along(axis, source, target):
-        return [send(source, target, axis, step) for step in range(1, sizes[axis])]
 
     def first(u):
         unit = units[u]
@@ -116,7 +121,7 @@
         own = wholes[unit.owner].at[(zi, yi, xi, ci) + unit.part()]
         copy = pltpu.make_async_copy(shard, own, local_sems.at[u])
         copy.start()
-        pending[u] = (copy, along(0, shard, own))
+        pending[u] = (copy, wires.along(0, shard, own))
 
     def settle(u):
         for copy in pending[u]:
@@ -131,8 +136,8 @@
         whole = wholes[unit.owner]
         pending[u] = []
         for half in range(unit.halves):
-            ref = whole.at[(slice(None), yi, xi, ci) + unit.part(half)]
-            pending[u] += along(2 - half, ref, ref)
+            ref = whole.at[(full, yi, xi, ci) + unit.part(half)]
+            pending[u] += wires.along(2 - half, ref, ref)
 
     def third(u):
         settle(u)
@@ -140,23 +145,456 @@
         whole = wholes[unit.owner]
         pending[u] = []
         for half in range(unit.halves):
-            index = (slice(None), yi, slice(None), ci) if half == 0 else (slice(None), slice(None), xi, ci)
+            index = (full, yi, full, ci) if half == 0 else (full, full, xi, ci)
             ref = whole.at[index + unit.part(half)]
-            pending[u] += along(1 + half, ref, ref)
+            pending[u] += wires.along(1 + half, ref, ref)
 
     def fourth(u):
         settle(u)
         unit = units[u]
-        ref = wholes[unit.owner].at[(slice(None), slice(None), slice(None), ci) + unit.part()]
-        pending[u] = along(3, ref, ref)
-
-    stages = (first, second, third, fourth, settle)
-    for tick in range(len(units) + len(stages) - 1):
-        for lag, stage in enumerate(stages):
-            if 0 <= tick - lag < len(units):
-                stage(tick - lag)
-    for copy in started:
-        copy.wait_send()
+        ref = wholes[unit.owner].at[(full, full, full, ci) + unit.part()]
+        pending[u] = wires.along(3, ref, ref)
+
+    return (first, second, third, fourth, settle)
+
+
+def mul(left, right, left_dim=1, right_dim=0):
+    return lax.dot_general(
+        left, right, (((left_dim,), (right_dim,)), ((), ())), preferred_element_type=jnp.float32
+    )
+
+
+def low(value):
+    return value.astype(jnp.bfloat16)
+
+
+def wide(value):
+    return value.astype(jnp.float32)
+
+
+def rms_rows(source, target, gain, rows=64):
+    def body(step, carry):
+        at = pl.ds(pl.multiple_of(step * rows, rows), rows)
+        value = wide(source[at, :])
+        scale = lax.rsqrt(jnp.mean(value * value, axis=-1, keepdims=True) + 1e-06)
+        target[at, :] = low(value * scale * gain)
+        return carry
+
+    lax.fori_loop(0, source.shape[0] // rows, body, 0)
+
+
+def tiles(total, size, body):
+    def step(spot, carry):
+        body(pl.ds(pl.multiple_of(spot * size, size), size))
+        return carry
+
+    lax.fori_loop(0, total // size, step, 0)
+
+
+def flat_rows(value):
+    return value.reshape(-1, value.shape[-1])
+
+
+def attend_pair(queries, key_rows, value_rows, bias, mask):
+    rows = queries.shape[0]
+    left = lax.broadcasted_iota(jnp.int32, (1, LANES), 1) < HEAD
+    zero = jnp.zeros_like(queries)
+    scaled = queries * jnp.bfloat16(HEAD ** (-0.5))
+    stacked = jnp.concatenate(
+        [jnp.where(left, scaled, zero), jnp.where(left, zero, scaled)], axis=0
+    )
+    scores = mul(stacked, key_rows, 1, 1)
+    if bias is not None:
+        scores = scores + bias
+    scores = jnp.where(mask, scores, -1e30)
+    powers = jnp.exp(scores - jnp.max(scores, axis=-1, keepdims=True))
+    probs = low(powers / jnp.sum(powers, axis=-1, keepdims=True))
+    none = jnp.zeros_like(value_rows)
+    mixed = mul(probs[:rows], jnp.where(left, value_rows, none)) + mul(
+        probs[rows:], jnp.where(left, none, value_rows)
+    )
+    return probs, low(mixed)
+
+
+class Driver:
+    def __init__(self, units, stages, lead):
+        self.units, self.stages, self.lead = units, stages, lead
+        self.tick, self.debt = 0, 0.0
+
+    def done(self):
+        return self.tick >= len(self.units) + len(self.stages) - 1
+
+    def settled(self):
+        return self.tick - len(self.stages)
+
+    def advance(self):
+        for lag, stage in enumerate(self.stages):
+            if 0 <= self.tick - lag < len(self.units):
+                stage(self.tick - lag)
+        self.tick += 1
+
+    def until(self, unit):
+        while self.settled() < unit:
+            self.advance()
+
+    def spent(self, cost):
+        self.debt += cost
+        while self.debt >= self.lead:
+            self.debt -= self.lead
+            if not self.done():
+                self.advance()
+
+
+KEPT = (
+    "normed_self", "qkv", "probs_self", "mixed_self", "second", "normed_cross", "queries", "pairs",
+    "probs_cross", "mixed_cross", "third", "normed_ffn", "branch", "hidden", "grad_gate_up",
+    "grad_normed", "gains",
+)
+CHUNK = 256
+ORDER = (0, 1, 2, 3, 4, 5, 7, 6)
+
+
+def forward_kernel(place, units, count, seqs, *refs):
+    shards, refs = refs[:count], refs[count:]
+    tokens, encoder, cotangent, lengths, enc_lengths, spread_ids = refs[:6]
+    wholes, refs = refs[6 : 6 + count], refs[6 + count :]
+    outcome, refs = refs[0], refs[1:]
+    stored, refs = refs[: len(KEPT)], refs[len(KEPT) :]
+    vmem, refs = dict(zip(KEPT, refs)), refs[len(KEPT) :]
+    bias_rows, slots, raw_out, ff_out, pack = refs[:5]
+    send_sems, recv_sems, local_sems, fetch_sems, keep_sems = refs[5:]
+    place.locate()
+    place.greet()
+    wires = Wires(place, send_sems, recv_sems)
+    driver = Driver(units, gather_stages(place, units, shards, wholes, wires, local_sems), 5.0)
+    rows, width = tokens.shape
+    slot_rows, enc_rows = rows // seqs, encoder.shape[0] // seqs
+    pairs_of_heads = width // LANES
+    norms = vmem["gains"].shape[0]
+    keeping = []
+
+    def keep(name):
+        copy = pltpu.make_async_copy(
+            vmem[name], stored[KEPT.index(name)], keep_sems.at[KEPT.index(name)]
+        )
+        copy.start()
+        keeping.append(copy)
+
+    first_of = {}
+    for u, unit in enumerate(units):
+        first_of.setdefault(unit.owner, u)
+    last_of = {unit.owner: u for u, unit in enumerate(units)}
+    slotted = [u for u, unit in enumerate(units) if unit.owner not in (0, 7)]
+    state = dict(fetched=0, used=0)
+    depth = slots.shape[0]
+
+    def fetch(u):
+        unit = units[u]
+        spot = slotted.index(u) % depth
+        return pltpu.make_async_copy(
+            wholes[unit.owner].at[(slice(None),) * 4 + unit.part()],
+            slots.at[(spot,) + (slice(None),) * 5 + (pl.ds(0, unit.shape[1]),)],
+            fetch_sems.at[spot],
+        )
+
+    def pump():
+        while (
+            state["fetched"] < len(slotted)
+            and slotted[state["fetched"]] <= driver.settled()
+            and state["fetched"] < state["used"] + depth
+        ):
+            fetch(slotted[state["fetched"]]).start()
+            state["fetched"] += 1
+
+    def spent(cost):
+        driver.spent(cost)
+        pump()
+
+    def weight(u):
+        driver.until(u)
+        pump()
+        fetch(u).wait()
+        spot = slotted.index(u) % depth
+        return lambda at: slots[spot, :, :, :, :, :, at].reshape(width, -1)
+
+    def release():
+        state["used"] += 1
+        pump()
+
+    def project(source, u, target, tile, cost):
+        matrix = weight(u)
+        size = units[u].shape[1]
+
+        def body(at):
+            target[:, at] = low(mul(source[...], matrix(at)))
+
+        tiles(size, tile, body)
+        release()
+        spent(cost)
+
+    def residual(source, u, before, target, cost):
+        matrix = weight(u)
+
+        def body(at):
+            target[:, at] = wide(before[:, at]) + mul(source[...], matrix(at))
+
+        tiles(width, CHUNK, body)
+        release()
+        spent(cost)
+
+    driver.until(0)
+    copy = pltpu.make_async_copy(wholes[0], pack, fetch_sems.at[depth])
+    copy.start()
+    copy.wait()
+    packs = wide(pack[...]).reshape(width // LANES, -1, PACK, LANES)
+    summed = jnp.sum(packs, axis=1)
+    for group in range(summed.shape[0]):
+        vmem["gains"][:, group * LANES : (group + 1) * LANES] = summed[group, :norms]
+    table = low(jnp.sum(summed, axis=0)[HEADS:, :BUCKETS])
+    spread = spread_ids[...]
+    onehot = (lax.broadcasted_iota(jnp.int32, (BUCKETS, spread.shape[1]), 0) == spread).astype(
+        jnp.bfloat16
+    )
+    bias_rows[...] = mul(table, onehot)
+    keep("gains")
+    rms_rows(tokens, vmem["normed_self"], vmem["gains"][0:1])
+    keep("normed_self")
+
+    for sequence in range(seqs):
+        at = pl.ds(sequence * slot_rows, slot_rows)
+        valid = lax.broadcasted_iota(jnp.int32, (slot_rows, 1), 0) < lengths[sequence]
+        vmem["branch"][at, :] = low(jnp.where(valid, wide(cotangent[at, :]), 0.0))
+    keep("branch")
+
+    for part in range(3):
+        project(vmem["normed_self"], first_of[1] + part, vmem["qkv"].at[part], CHUNK, 2.0)
+    keep("qkv")
+    for part in range(2):
+        project(encoder, first_of[2] + part, vmem["pairs"].at[part], CHUNK, 3.0)
+    keep("pairs")
+
+    def self_pair(pair, carry):
+        lanes = pl.ds(pl.multiple_of(pair * LANES, LANES), LANES)
+        row = lax.broadcasted_iota(jnp.int32, (slot_rows, slot_rows), 0)
+        column = lax.broadcasted_iota(jnp.int32, (slot_rows, slot_rows), 1)
+        period = bias_rows.shape[1]
+        bias = jnp.concatenate(
+            [
+                pltpu.roll(
+                    jnp.broadcast_to(bias_rows[2 * pair + head, :][None], (slot_rows, period)),
+                    0,
+                    1,
+                    stride=1,
+                    stride_axis=0,
+                )[:, :slot_rows]
+                for head in range(2)
+            ],
+            axis=0,
+        )
+        for sequence in range(seqs):
+            at = pl.ds(sequence * slot_rows, slot_rows)
+            mask = (column <= row) & (column < lengths[sequence])
+            probs, mixed = attend_pair(
+                vmem["qkv"][0, at, lanes],
+                vmem["qkv"][1, at, lanes],
+                vmem["qkv"][2, at, lanes],
+                bias,
+                jnp.concatenate([mask, mask], axis=0),
+            )
+            vmem["probs_self"][sequence, pair] = probs
+            vmem["mixed_self"][at, lanes] = mixed
+        return carry
+
+    for pair in range(0, pairs_of_heads, 2):
+        lax.fori_loop(pair, pair + 2, self_pair, 0)
+        spent(3.0)
+    keep("probs_self")
+    keep("mixed_self")
+    residual(vmem["mixed_self"], first_of[3], tokens, vmem["second"], 1.0)
+    keep("second")
+    rms_rows(vmem["second"], vmem["normed_cross"], vmem["gains"][1:2])
+    keep("normed_cross")
+    project(vmem["normed_cross"], first_of[4], vmem["queries"], CHUNK, 2.0)
+    keep("queries")
+
+    def cross_pair(pair, carry):
+        lanes = pl.ds(pl.multiple_of(pair * LANES, LANES), LANES)
+        column = lax.broadcasted_iota(jnp.int32, (1, enc_rows), 1)
+        for sequence in range(seqs):
+            at = pl.ds(sequence * slot_rows, slot_rows)
+            keys = pl.ds(sequence * enc_rows, enc_rows)
+            probs, mixed = attend_pair(
+                vmem["queries"][at, lanes],
+                vmem["pairs"][0, keys, lanes],
+                vmem["pairs"][1, keys, lanes],
+                None,
+                column < enc_lengths[sequence],
+            )
+            vmem["probs_cross"][sequence, pair] = probs
+            vmem["mixed_cross"][at, lanes] = mixed
+        return carry
+
+    for pair in range(0, pairs_of_heads, 2):
+        lax.fori_loop(pair, pair + 2, cross_pair, 0)
+        spent(4.0)
+    keep("probs_cross")
+    keep("mixed_cross")
+    residual(vmem["mixed_cross"], first_of[5], vmem["second"], vmem["third"], 1.0)
+    keep("third")
+    rms_rows(vmem["third"], vmem["normed_ffn"], vmem["gains"][2:3])
+    keep("normed_ffn")
+
+    driver.until(last_of[7])
+    copy = pltpu.make_async_copy(wholes[7], raw_out, fetch_sems.at[depth])
+    copy.start()
+    copy.wait()
+    sizes = place.sizes
+    joined = 2 * raw_out.shape[4] * 8
+
+    def unpack(step, carry):
+        at = (step // (sizes[1] * sizes[2]), (step // sizes[2]) % sizes[1], step % sizes[2])
+        ff_out[pl.ds(pl.multiple_of(step * joined, 16), joined), :] = low(
+            wide(raw_out[at]).reshape(joined, width)
+        )
+        return carry
+
+    lax.fori_loop(0, sizes[0] * sizes[1] * sizes[2], unpack, 0)
+    spent(3.0)
+    outcome[...] = vmem["third"][...]
+    vmem["grad_normed"][...] = jnp.zeros_like(vmem["grad_normed"])
+
+    def ffn_chunk(matrix, chunk, lane):
+        gate_at = pl.ds(pl.multiple_of(lane, 2 * CHUNK), CHUNK)
+        up_at = pl.ds(pl.multiple_of(lane + CHUNK, CHUNK), CHUNK)
+        normed = vmem["normed_ffn"][...]
+        gate = mul(normed, matrix(gate_at))
+        up = mul(normed, matrix(up_at))
+        square = gate * gate
+        curve = jnp.tanh(0.7978845608028654 * gate * (1.0 + 0.044715 * square))
+        half = 0.5 * (1.0 + curve)
+        gelu = gate * half
+        slope = half + 0.5 * gate * (1.0 - curve * curve) * (
+            0.7978845608028654 * (1.0 + 3 * 0.044715 * square)
+        )
+        hidden = low(gelu * up)
+        vmem["hidden"][chunk] = hidden
+        down_at = pl.ds(pl.multiple_of(chunk * CHUNK, CHUNK), CHUNK)
+        grad_hidden = mul(vmem["branch"][...], ff_out[down_at, :], 1, 1)
+        grads = jnp.concatenate([low(grad_hidden * up * slope), low(grad_hidden * gelu)], axis=1)
+        vmem["grad_gate_up"][chunk] = grads
+
+        def add_out(at):
+            outcome[:, at] += mul(vmem["hidden"][chunk], ff_out[down_at, at])
+
+        tiles(width, CHUNK, add_out)
+
+        def add_back(at):
+            vmem["grad_normed"][at, :] += mul(
+                vmem["grad_gate_up"][chunk, at, :],
+                matrix(pl.ds(pl.multiple_of(lane, 2 * CHUNK), 2 * CHUNK)),
+                1,
+                1,
+            )
+
+        tiles(rows, LANES, add_back)
+
+    chunk = 0
+    for u in range(first_of[6], last_of[6] + 1):
+        matrix = weight(u)
+        inside = units[u].shape[1] // (2 * CHUNK)
+
+        def step(spot, carry, matrix=matrix, chunk=chunk):
+            ffn_chunk(matrix, chunk + spot, spot * 2 * CHUNK)
+            return carry
+
+        lax.fori_loop(0, inside, step, 0)
+        chunk += inside
+        release()
+        spent(3.0 * inside)
+    for name in ("hidden", "grad_gate_up", "grad_normed"):
+        keep(name)
+    while not driver.done():
+        driver.advance()
+    for copy in keeping:
+        copy.wait()
+    wires.finish()
+
+
+def kept_shapes(seqs, slot_rows, enc_rows, width, hidden, norms):
+    rows = seqs * slot_rows
+    pairs = width // LANES
+    low_type, wide_type = jnp.bfloat16, jnp.float32
+    return {
+        "normed_self": ((rows, width), low_type),
+        "qkv": ((3, rows, width), low_type),
+        "probs_self": ((seqs, pairs, 2 * slot_rows, slot_rows), low_type),
+        "mixed_self": ((rows, width), low_type),
+        "second": ((rows, width), wide_type),
+        "normed_cross": ((rows, width), low_type),
+        "queries": ((rows, width), low_type),
+        "pairs": ((2, seqs * enc_rows, width), low_type),
+        "probs_cross": ((seqs, pairs, 2 * slot_rows, enc_rows), low_type),
+        "mixed_cross": ((rows, width), low_type),
+        "third": ((rows, width), wide_type),
+        "normed_ffn": ((rows, width), low_type),
+        "branch": ((rows, width), low_type),
+        "hidden": ((hidden // CHUNK, rows, CHUNK), low_type),
+        "grad_gate_up": ((hidden // CHUNK, rows, 2 * CHUNK), low_type),
+        "grad_normed": ((rows, width), wide_type),
+        "gains": ((norms, width), wide_type),
+    }
+
+
+def forward_all(place, shards, tokens, encoder, cotangent, lengths, enc_lengths, bucket_ids, norms):
+    blocks = [shard.shape for shard in shards]
+    units = make_units(blocks, PIECE, ORDER)
+    total = copies_of(units, place.sizes, False)
+    anywhere = pl.BlockSpec(memory_space=pl.ANY)
+    inside = pl.BlockSpec(memory_space=pltpu.VMEM)
+    scalars = pl.BlockSpec(memory_space=pltpu.SMEM)
+    seqs, slot_rows, width = tokens.shape
+    rows = seqs * slot_rows
+    hidden = blocks[6][1] // 2
+    kept = kept_shapes(seqs, slot_rows, encoder.shape[1], width, hidden, norms)
+    spread = jnp.concatenate(
+        [bucket_ids[:1], jnp.broadcast_to(bucket_ids[:1], (slot_rows,)), bucket_ids[:0:-1]]
+    )[None]
+    depth = 3
+    results = pl.pallas_call(
+        functools.partial(forward_kernel, place, units, len(blocks), seqs),
+        out_shape=[jax.ShapeDtypeStruct(place.sizes + block, jnp.bfloat16) for block in blocks]
+        + [jax.ShapeDtypeStruct((rows, width), jnp.float32)]
+        + [jax.ShapeDtypeStruct(*kept[name]) for name in KEPT],
+        in_specs=[anywhere] * len(blocks) + [inside] * 3 + [scalars] * 2 + [inside],
+        out_specs=[anywhere] * len(blocks) + [inside] + [anywhere] * len(KEPT),
+        scratch_shapes=[pltpu.VMEM(*kept[name]) for name in KEPT]
+        + [
+            pltpu.VMEM((HEADS, 2 * slot_rows), jnp.float32),
+            pltpu.VMEM((depth,) + place.sizes + (blocks[1][0], PIECE // blocks[1][0]), jnp.bfloat16),
+            pltpu.VMEM(place.sizes + blocks[7], jnp.bfloat16),
+            pltpu.VMEM((hidden, width), jnp.bfloat16),
+            pltpu.VMEM(place.sizes + blocks[0], jnp.bfloat16),
+            pltpu.SemaphoreType.DMA((total,)),
+            pltpu.SemaphoreType.DMA((total,)),
+            pltpu.SemaphoreType.DMA((len(units),)),
+            pltpu.SemaphoreType.DMA((depth + 1,)),
+            pltpu.SemaphoreType.DMA((len(KEPT),)),
+        ],
+        compiler_params=pltpu.CompilerParams(
+            collective_id=0, has_side_effects=True, vmem_limit_bytes=63 * 2**20
+        ),
+        name="forward_all",
+    )(
+        *shards,
+        tokens.reshape(rows, width),
+        encoder.reshape(-1, width),
+        cotangent.reshape(rows, width),
+        lengths,
+        enc_lengths,
+        spread,
+    )
+    count = len(blocks)
+    return results[:count], results[count], dict(zip(KEPT, results[count + 1 :]))
 
 
 def scatter_kernel(place, units, count, slot_of, *refs):
@@ -314,27 +752,8 @@
     return total
 
 
-def gather_all(place, blocks, shards):
-    units = make_units(blocks, PIECE)
-    total = copies_of(units, place.sizes, False)
-    anywhere = pl.BlockSpec(memory_space=pl.ANY)
-    return pl.pallas_call(
-        functools.partial(gather_kernel, place, units, len(blocks)),
-        out_shape=[jax.ShapeDtypeStruct(place.sizes + block, jnp.bfloat16) for block in blocks],
-        in_specs=[anywhere] * len(blocks),
-        out_specs=[anywhere] * len(blocks),
-        scratch_shapes=[
-            pltpu.SemaphoreType.DMA((total,)),
-            pltpu.SemaphoreType.DMA((total,)),
-            pltpu.SemaphoreType.DMA((len(units),)),
-        ],
-        compiler_params=pltpu.CompilerParams(collective_id=0, has_side_effects=True),
-        name="gather_all",
-    )(*shards)
-
-
 def scatter_all(place, blocks, wholes):
-    units = make_units(blocks, PIECE)
+    units = make_units(blocks, PIECE, ORDER)
     sizes = place.sizes
     total = copies_of(units, sizes, True)
     scratch, kinds, slot_of = [], [], []
@@ -560,6 +979,89 @@
     )
 
 
+def back(kept, weights, gains, data):
+    self_qkv, cross_kv, self_out, cross_q, cross_out, ff_in, ff_out = weights
+    tokens, encoder, cotangent, lengths, enc_lengths, bucket_ids = data
+    count, slots, width = tokens.shape
+    enc_count = encoder.shape[1]
+    heads = lambda a, n: a.reshape(count, n, HEADS, HEAD)
+    probs_of = lambda a: a.reshape(count, HEADS, slots, -1)
+    bucket_map = toeplitz(bucket_ids, slots).reshape(-1)
+    onehot = (lax.iota(jnp.int32, BUCKETS)[:, None] == bucket_map[None, :]).astype(jnp.bfloat16)
+    enc_rows = encoder.reshape(count * enc_count, width)
+    low = lambda value: value.astype(jnp.bfloat16)
+    stream = tokens.reshape(count * slots, width).astype(jnp.float32)
+    unused, back_self = jax.vjp(norm_scale, stream, gains[0])
+    unused, back_cross = jax.vjp(norm_scale, kept["second"], gains[1])
+    unused, back_ffn = jax.vjp(norm_scale, kept["third"], gains[2])
+    hidden = kept["hidden"].transpose(1, 0, 2).reshape(count * slots, -1)
+    grad_gate_up = kept["grad_gate_up"].transpose(1, 0, 2).reshape(count * slots, -1)
+    row_ids = lax.iota(jnp.int32, slots)
+    valid = (row_ids[None, :] < lengths[:, None]).astype(jnp.float32)[:, :, None]
+    grad_out = (cotangent.astype(jnp.float32) * valid).reshape(count * slots, width)
+    grad_ff_out = product("lf,ld->fd", hidden, kept["branch"])
+    grad_ff_in = product("ld,lf->df", kept["normed_ffn"], grad_gate_up)
+    grad_stream, gain_ffn = back_ffn(kept["grad_normed"])
+    grad_third = grad_out + grad_stream
+    branch = low(grad_third)
+    grad_cross_out = product("le,ld->ed", kept["mixed_cross"], branch)
+    grad_mixed = heads(low(product("ld,ed->le", branch, cross_out)), slots)
+    grad_queries, grad_keys, grad_values, unused = attend_back(
+        heads(kept["queries"], slots),
+        heads(kept["pairs"][0], enc_count),
+        heads(kept["pairs"][1], enc_count),
+        probs_of(kept["probs_cross"]),
+        grad_mixed,
+    )
+    grad_query_rows = low(grad_queries.reshape(count * slots, width))
+    grad_pair_rows = low(
+        jnp.concatenate(
+            [
+                grad_keys.reshape(count * enc_count, width),
+                grad_values.reshape(count * enc_count, width),
+            ],
+            axis=1,
+        )
+    )
+    grad_cross_q = product("ld,le->de", kept["normed_cross"], grad_query_rows)
+    grad_cross_kv = product("ed,ef->df", enc_rows, grad_pair_rows)
+    grad_enc = product("ef,df->ed", grad_pair_rows, cross_kv)
+    grad_stream, gain_cross = back_cross(product("le,de->ld", grad_query_rows, cross_q))
+    grad_second = grad_third + grad_stream
+    branch = low(grad_second)
+    grad_self_out = product("le,ld->ed", kept["mixed_self"], branch)
+    grad_mixed = heads(low(product("ld,ed->le", branch, self_out)), slots)
+    grad_queries, grad_keys, grad_values, grad_scores = attend_back(
+        heads(kept["qkv"][0], slots),
+        heads(kept["qkv"][1], slots),
+        heads(kept["qkv"][2], slots),
+        probs_of(kept["probs_self"]),
+        grad_mixed,
+    )
+    score_sums = jnp.sum(grad_scores.astype(jnp.float32), axis=0).reshape(HEADS, slots * slots)
+    grad_rel_bias = product("hn,bn->hb", low(score_sums), onehot)
+    grad_qkv = low(
+        jnp.concatenate(
+            [part.reshape(count * slots, width) for part in (grad_queries, grad_keys, grad_values)],
+            axis=1,
+        )
+    )
+    grad_self_qkv = product("ld,lf->df", kept["normed_self"], grad_qkv)
+    grad_stream, gain_self = back_self(product("lf,df->ld", grad_qkv, self_qkv))
+    grad_tok = grad_second + grad_stream
+    grad_gains = jnp.stack([gain_self, gain_cross, gain_ffn], axis=0)
+    grads = (
+        grad_self_qkv,
+        grad_cross_kv,
+        grad_self_out,
+        grad_cross_q,
+        grad_cross_out,
+        grad_ff_in,
+        grad_ff_out,
+    )
+    return grad_tok.reshape(tokens.shape), grad_enc.reshape(encoder.shape), grads, grad_gains, grad_rel_bias
+
+
 def by_kernels(place, data, shards):
     norm_gains, rel_bias = shards[7:]
     count = place.sizes[0] * place.sizes[1] * place.sizes[2] * place.sizes[3]
@@ -573,19 +1075,20 @@
     pack = lax.dynamic_update_slice(pack, rel_bias.reshape(1, rel_per), (rel_row, rel_column))
     ff_rows, width = shards[6].shape
     ff_shape = (ff_rows // 8, 8, width)
-    sent = (pack,) + shards[:6] + (shards[6].reshape(ff_shape),)
+    self_qkv, self_out, cross_q, cross_kv, cross_out, ff_in, ff_out = shards[:7]
+    chunks = ff_in.shape[1] // (2 * CHUNK)
+    laced = ff_in.reshape(-1, 2, chunks, CHUNK).transpose(0, 2, 1, 3).reshape(ff_in.shape)
+    sent = (pack, self_qkv, cross_kv, self_out, cross_q, cross_out, laced, ff_out.reshape(ff_shape))
     blocks = [piece.shape for piece in sent]
-    packs, *wholes = gather_all(place, blocks, sent)
+    wholes, outcome, kept = forward_all(place, sent, *data, norms)
     weights = tuple(
         whole.reshape(count * shard.shape[0], shard.shape[1])
-        for whole, shard in zip(wholes, shards[:7])
-    )
-    packs = packs.reshape(count // group, group, PACK, LANES).astype(jnp.float32).sum(axis=1)
-    gains = packs[:, :norms].transpose(1, 0, 2).reshape(norms, -1)
-    rel_table = packs.sum(axis=0)[HEADS:, :BUCKETS].astype(jnp.bfloat16)
-    outcome, grad_tok, grad_enc, grads, grad_gains, grad_rel_bias = layer(
-        weights, gains, rel_table, *data
-    )
+        for whole, shard in zip(
+            wholes[1:], (self_qkv, cross_kv, self_out, cross_q, cross_out, ff_in, ff_out)
+        )
+    )
+    outcome = outcome.reshape(data[0].shape)
+    grad_tok, grad_enc, grads, grad_gains, grad_rel_bias = back(kept, weights, kept["gains"], data)
     top = grad_gains.reshape(norms, count // group, LANES).transpose(1, 0, 2)
     top = jnp.pad(top, ((0, 0), (0, HEADS - norms), (0, 0)))
     low_part = jnp.pad(grad_rel_bias, ((0, 0), (0, LANES - BUCKETS)))
@@ -600,10 +1103,11 @@
             for piece, block in zip((tiles,) + grads, blocks)
         ],
     )
-    packed, *owned = sums
+    packed, g_qkv, g_kv, g_so, g_cq, g_co, g_in, g_out = sums
+    g_in = g_in.reshape(-1, chunks, 2, CHUNK).transpose(0, 2, 1, 3).reshape(ff_in.shape)
+    owned = [g_qkv, g_so, g_cq, g_kv, g_co, g_in, g_out.reshape(ff_rows, width)]
     own_gains = lax.dynamic_slice(packed, (0, (me % group) * per), (norms, per))
     own_rel = lax.dynamic_slice(packed, (rel_row, rel_column), (1, rel_per)).reshape(-1)
-    owned[6] = owned[6].reshape(ff_rows, width)
     return (outcome, grad_tok, grad_enc) + tuple(owned) + (own_gains, own_rel)
 
 

time: 666 us -> 569 us (0.85)
  matrix products: 161 us -> 89.2 us
  Pallas kernels: 322 us -> 349 us
  other arithmetic: 41.7 us -> 15.4 us
  local copies, waits for them, and re-layouts: 130 us -> 104 us
    dot_general x8 -> x0, matrix products: 36.4 us -> none  [the longest x1 8.2 us: layer(): gate_up = dot(normed_ffn, ff_in)]
    dot_general x27 -> x21, matrix products: 124 us -> 89.2 us  [product(): return jnp.einsum(spec, left, right, preferred_element_type=jnp.float32)]
    pallas_call x1, Pallas kernels: 159 us -> 188 us  [forward_all(): pl.pallas_call(functools.partial(forward_kernel, place, units, len(blocks...]
    sub x2 -> x0, other arithmetic: 19.7 us -> none  [attend(): powers = jnp.exp(masked - row_max)]
    another operation x3 -> x8, local copies, waits for them, and re-layouts: 3.25 us -> 21.6 us  [the longest x5 18.3 us: back(): heads = lambda a, n: a.reshape(count, n, HEADS, HEAD)]
    reshape x13 -> x14, local copies, waits for them, and re-layouts: 46.8 us -> 30.6 us  [the longest x5 14.4 us: back(): heads = lambda a, n: a.reshape(count, n, HEADS, HEAD)]
    unnamed x136 -> x113, local copies, waits for them, and re-layouts: 26.2 us -> 10.5 us
    transpose x1 -> x3, local copies, waits for them, and re-layouts: 0.01 us -> 9.41 us  [the longest x1 6.75 us: back(): kept['grad_gate_up'].transpose(1, 0, 2).reshape(count * slots, -1)]
where the time goes in v2:
time: 569 us; the launch traced here: 559 us
  Pallas kernels  349 us (61%)
  local copies, waits for them, and re-layouts  104 us (18%)
  matrix products  89.2 us (16%)
  other arithmetic  15.4 us (3%)
    pallas_call x1, Pallas kernels, forward_all(): pl.pallas_call(functools.partial(forward_kernel, place, units, len(blocks...  188 us
    pallas_call x1, Pallas kernels, scatter_all(): pl.pallas_call(functools.partial(scatter_kernel, place, units, len(blocks...  162 us
    dot_general x21, matrix products, product(): return jnp.einsum(spec, left, right, preferred_element_type=jnp.float32)  89.2 us
    another operation x5, local copies, waits for them, and re-layouts, back(): heads = lambda a, n: a.reshape(count, n, HEADS, HEAD)  18.3 us
    reshape x5, local copies, waits for them, and re-layouts, back(): heads = lambda a, n: a.reshape(count, n, HEADS, HEAD)  14.4 us

profile of v2, /device:TPU:0, one launch (start us, length us, event | category | flops | bytes accessed | tf_op | source)
XLA Modules:
  0.0 559.2 jit_solution(4814461787015746737)
XLA Ops:
  9.6 187.6 %forward_all.1 = (bf16[4,2,2,2,32,128]{5,4,3,2,1,0:T(8,128)(2,1)}, bf16[4,2,2,2,32,3072]{5,4,3,2,1,0:T(8,128)(2,1)}, bf16[4,2,2,2,32,2048]{5,4,3,2,1,0:T(8,128)(...) custom-call(bf16[32,128]{1,0:T(8,128)(2,1)} %copy-done.36, ...), custom_call_target="tpu_custom_call" | custom-call | tf_op jit(solution)/shard_map/forward_all/pallas_call | solution.py:563
  209.2 3.8 fusion.50
  213.0 5.4 reshape.313
  218.4 6.8 %fusion = (f32[2,16,192]{2,1,0:T(8,128)S(1)}, f32[2,16,192,384]{3,2,1,0:T(8,128)S(1)}) fusion(bf16[2,16,192,384]{3,2,1,0:T(8,128)(2,1)} %bitcast.120, bf16[2,192,16,64]{1,3,2,0:T(8,128)(2,1)S(1)} %copy.116, bf16[2,384,16,64]{3,2,1,0:T(8,128)(2,1)} %reshape.313), kind=kOutput, calls=%fused_computation.3 | convolution fusion | flops 309061632 | bytes 16539648 | tf_op jit(solution)/shard_map/bihc,bjhc->bhij/dot_general | solution.py:816
  225.2 3.3 fusion.1
  228.5 3.3 reshape.317
  231.8 4.3 multiply_convert_fusion
  242.4 6.7 %convolution_convert_fusion.3 = bf16[2048,1024]{0,1:T(8,128)(2,1)} fusion(bf16[768,1024]{1,0:T(8,128)(2,1)S(1)} %bitcast.154, bf16[768,1024]{0,1:T(8,128)(2,1)S(1)} %bitcast.152, bf16[768,1024]{0,1:T(8,128)(2,1)S(1)} %bitcast.151), kind=kOutput, calls=%fused_computation.13 | convolution fusion | flops 3229614080 | bytes 8912896 | tf_op jit(solution)/shard_map/ed,ef->df/dot_general | solution.py:816
  249.2 5.2 reshape.312
  254.4 5.4 fusion.31
  262.4 3.7 multiply_reduce_fusion.1
  274.4 3.4 reshape.319
  277.8 3.5 copy.124
  289.1 3.4 copy.121
  295.3 4.7 fusion.48
  307.6 3.7 reshape.288
  311.3 3.4 reshape.314
  319.8 5.5 convolution_convert_fusion.2
  325.6 7.6 %fusion.23 = (bf16[1024]{0:T(1024)(128)(2,1)S(1)}, f32[384]{0:T(512)S(1)}, f32[384,1024]{1,0:T(8,128)}) fusion(f32[384]{0:T(512)S(1)} %rsqrt.32, bf16[2,192,1024]{2,1,0:T(8,128)(2,1)S(1)} %copy-done.11, f32[1024]{0:T(1024)S(1)} %bitcast.163, bf16[384,3072]{0,1:T(8,128)(2,1)} %copy-done.31, bf16[1024,3072]{1,0:T(8,128)(2,1)} %bitcast.171), kind=kOutput, calls=%fused_computation.44 | convolution fusion | flops 2418670080 | bytes 11019264 | tf_op jit(solution)/shard_map/lf,df->ld/dot_general | solution.py:816
  341.2 6.7 %copy.144 = bf16[384,11,512]{0,2,1:T(8,128)(2,1)} copy(bf16[384,11,512]{2,0,1:T(8,128)(2,1)} %bitcast.141) | data formatting | bytes 8650752 | tf_op jit(solution)/shard_map/transpose | solution.py:998
  347.9 11.5 %convolution_convert_fusion = bf16[1024,5632]{1,0:T(8,128)(2,1)} fusion(bf16[384,1024]{1,0:T(8,128)(2,1)S(1)} %copy-done.42, bf16[384,5632]{0,1:T(8,128)(2,1)} %bitcast.142), kind=kOutput, calls=%fused_computation.2 | convolution fusion | flops 4434952192 | bytes 16646144 | tf_op jit(solution)/shard_map/ld,lf->df/dot_general | solution.py:816
  361.8 6.7 %convolution_convert_fusion.1 = bf16[2816,1024]{1,0:T(8,128)(2,1)} fusion(bf16[384,2816]{0,1:T(8,128)(2,1)} %bitcast.147, bf16[384,1024]{1,0:T(8,128)(2,1)S(1)} %copy-done.41), kind=kOutput, calls=%fused_computation.9 | convolution fusion | flops 2217476096 | bytes 8716288 | tf_op jit(solution)/shard_map/lf,ld->fd/dot_general | solution.py:816
  371.2 161.6 %scatter_all.1 = (f32[32,128]{1,0:T(8,128)}, f32[32,3072]{1,0:T(8,128)}, f32[32,2048]{1,0:T(8,128)}, f32[32,1024]{1,0:T(8,128)}, f32[32,1024]{1,0:T(8,128)}, /*i...) custom-call(bf16[4,2,2,2,32,128]{5,4,3,2,1,0:T(8,128)(2,1)} %broadcast_in_dim.58.refs_0_, ...), custom_call_target="tpu_custom_call" | custom-call | tf_op jit(solution)/shard_map/scatter_all/pallas_call | solution.py:779
  543.9 7.9 %fusion.5 = f32[2,384,1024]{2,1,0:T(8,128)} fusion(bf16[1024,2048,1]{1,0,2:T(8,128)(2,1)} %bitcast.172, bf16[2,384,1024]{2,1,0:T(8,128)(2,1)} %copy.139, bf16[2,384,1024]{2,1,0:T(8,128)(2,1)S(1)} %copy-done.23), kind=kOutput, calls=%fused_computation.14 | convolution fusion | flops 3227516928 | bytes 10485760 | tf_op jit(solution)/shard_map/ef,df->ed/dot_general | solution.py:816
  (193 shorter events, 92.4 us)
Async XLA Ops:
  3.0 6.6 %copy-start.36 = (bf16[32,128]{1,0:T(8,128)(2,1)}, bf16[32,128]{1,0:T(8,128)(2,1)S(1)}, u32[]{:S(2)}) copy-start(bf16[32,128]{1,0:T(8,128)(2,1)S(1)} %dynamic_update_slice.7.refs_0_) | copy-start | bytes 24580
  198.1 3.8 copy-start.19
  202.7 63.4 %copy-start.3 = (f32[384,1024]{1,0:T(8,128)}, f32[384,1024]{1,0:T(8,128)S(1)}, u32[]{:S(2)}) copy-start(f32[384,1024]{1,0:T(8,128)S(1)} %get-tuple-element.96) | copy-start | bytes 4718596
  218.4 6.8 %slice-start = ((s8[4718592]{0:T(1024)(128)(4,1)}), s8[4194304]{0:T(1024)(128)(4,1)S(1)}, s32[]{:S(2)}) async-start(s8[4718592]{0:T(1024)(128)(4,1)} %bitcast.121), calls=%async_computation | async-start | bytes 8388608
  218.4 6.8 %slice-start.1 = ((s8[4718592]{0:T(1024)(128)(4,1)}), s8[524288]{0:T(1024)(128)(4,1)S(1)}, s32[]{:S(2)}) async-start(s8[4718592]{0:T(1024)(128)(4,1)} %bitcast.121), calls=%async_computation.1 | async-start | bytes 1048576
  228.5 9.6 %slice-start.2 = ((s8[4718592]{0:T(1024)(128)(4,1)}), s8[524288]{0:T(1024)(128)(4,1)S(1)}, s32[]{:S(2)}) async-start(s8[4718592]{0:T(1024)(128)(4,1)} %bitcast.124), calls=%async_computation.2 | async-start | bytes 1048576
  231.8 6.3 %slice-start.3 = ((s8[4718592]{0:T(1024)(128)(4,1)}), s8[4194304]{0:T(1024)(128)(4,1)S(1)}, s32[]{:S(2)}) async-start(s8[4718592]{0:T(1024)(128)(4,1)} %bitcast.124), calls=%async_computation.3 | async-start | bytes 8388608
  266.5 6.0 %copy-start.6 = (f32[384,1024]{1,0:T(8,128)}, f32[384,1024]{1,0:T(8,128)S(1)}, u32[]{:S(2)}) copy-start(f32[384,1024]{1,0:T(8,128)S(1)} %fusion.20) | copy-start | bytes 4718596
  274.4 6.9 %copy-start.10 = (bf16[2,8,384,192]{3,2,1,0:T(8,128)(2,1)S(1)}, bf16[2,8,384,192]{3,2,1,0:T(8,128)(2,1)}, u32[]{:S(2)}) copy-start(bf16[2,8,384,192]{3,2,1,0:T(8,128)(2,1)} %get-tuple-element.53) | copy-start | bytes 7077892
  307.6 7.0 %copy-start = (bf16[2,16,192,192]{2,3,1,0:T(8,128)(2,1)S(1)}, bf16[2,16,192,192]{2,3,1,0:T(8,128)(2,1)}, u32[]{:S(2)}) copy-start(bf16[2,16,192,192]{2,3,1,0:T(8,128)(2,1)} %get-tuple-element.81) | copy-start | bytes 7077892
  319.5 5.7 %copy-start.31 = (bf16[384,3072]{0,1:T(8,128)(2,1)}, bf16[384,3072]{0,1:T(8,128)(2,1)S(1)}, u32[]{:S(2)}) copy-start(bf16[384,3072]{0,1:T(8,128)(2,1)S(1)} %constant_dynamic-update-slice_fusion) | copy-start | bytes 7077892
  319.8 5.5 copy-start.11
  325.6 7.6 %copy-start.15 = (bf16[16,192,192]{1,2,0:T(8,128)(2,1)S(1)}, bf16[16,192,192]{1,2,0:T(8,128)(2,1)}, u32[]{:S(2)}) copy-start(bf16[16,192,192]{1,2,0:T(8,128)(2,1)} %get-tuple-element.80) | copy-start | bytes 3538948
  341.1 6.8 %copy-start.42 = (bf16[384,1024]{1,0:T(8,128)(2,1)S(1)}, bf16[384,1024]{1,0:T(8,128)(2,1)}, u32[]{:S(2)}) copy-start(bf16[384,1024]{1,0:T(8,128)(2,1)} %get-tuple-element.62) | copy-start | bytes 2359300
  347.9 11.6 %copy-start.21 = (bf16[11,384,256]{2,1,0:T(8,128)(2,1)S(1)}, bf16[11,384,256]{2,1,0:T(8,128)(2,1)}, u32[]{:S(2)}) copy-start(bf16[11,384,256]{2,1,0:T(8,128)(2,1)} %get-tuple-element.64) | copy-start | bytes 6488068
  361.8 6.7 %copy-start.4 = (f32[384,1024]{1,0:T(8,128)S(1)}, f32[384,1024]{1,0:T(8,128)}, u32[]{:S(2)}) copy-start(f32[384,1024]{1,0:T(8,128)} %copy-done.3) | copy-start | bytes 4718596
  361.8 6.7 %copy-start.27 = (bf16[384,1024]{1,0:T(8,128)(2,1)S(1)}, bf16[384,1024]{1,0:T(8,128)(2,1)}, u32[]{:S(2)}) copy-start(bf16[384,1024]{1,0:T(8,128)(2,1)} %get-tuple-element.61) | copy-start | bytes 2359300
  534.3 6.1 %copy-start.9 = (bf16[2,16,64,384]{3,2,1,0:T(8,128)(2,1)S(1)}, bf16[2,16,64,384]{3,2,1,0:T(8,128)(2,1)}, u32[]{:S(2)}) copy-start(bf16[2,16,64,384]{3,2,1,0:T(8,128)(2,1)} %copy-done.8) | copy-start | bytes 4718596
  535.4 6.6 %copy-start.2 = (bf16[2,16,64,384]{3,2,1,0:T(8,128)(2,1)S(1)}, bf16[2,16,64,384]{3,2,1,0:T(8,128)(2,1)}, u32[]{:S(2)}) copy-start(bf16[2,16,64,384]{3,2,1,0:T(8,128)(2,1)} %copy-done.1) | copy-start | bytes 4718596
  543.9 8.0 %copy-start.7 = (f32[384,1024]{1,0:T(8,128)S(1)}, f32[384,1024]{1,0:T(8,128)}, u32[]{:S(2)}) copy-start(f32[384,1024]{1,0:T(8,128)} %copy-done.6) | copy-start | bytes 4718596
  543.9 8.0 %copy-start.12 = (bf16[2,192,1024]{2,1,0:T(8,128)(2,1)S(1)}, bf16[2,192,1024]{2,1,0:T(8,128)(2,1)}, u32[]{:S(2)}) copy-start(bf16[2,192,1024]{2,1,0:T(8,128)(2,1)} %param.15) | copy-start | bytes 2359300
  543.9 8.0 %copy-start.25 = (f32[384,1024]{1,0:T(8,128)S(1)}, f32[384,1024]{1,0:T(8,128)}, u32[]{:S(2)}) copy-start(f32[384,1024]{1,0:T(8,128)} %get-tuple-element.95) | copy-start | bytes 4718596
  553.5 3.9 copy-start.33
  553.5 4.6 copy-start.30
  (25 other events, 54.9 us)
